TPU v7x, 512 devices: a whole 4x8x8 slice. The times are simulated.
512 devices in a mesh: leaf: 8 (over z), rows: 64 (over y, x, core).
Axes of the slice: x: 4, y: 8, z: 8, core: 2. Of those that a mesh axis runs over, the one named last changes fastest.
Arguments:
- right_side: float32 [64, 196608], P(None, ('leaf', 'rows')), may hold values from -6 to 6
- tip_tags: int32 [196608], P(('leaf', 'rows')), may hold values from 0 to 2
- leaf_blocks: bfloat16 [3, 384, 196608], P(None, None, ('leaf', 'rows')), may hold values from -0.1875 to 0.1875
- leaf_cols: int32 [512, 2], P(('leaf', 'rows')), may hold values from 0 to 63
- u_panels: bfloat16 [3, 256, 196608], P(None, None, ('leaf', 'rows')), may hold values from -0.375 to 0.375
- v_panels: bfloat16 [3, 256, 196608], P(None, None, ('leaf', 'rows')), may hold values from -0.0390625 to 0.0390625
- cap_top: bfloat16 [2, 256, 512], replicated, may hold values from -0.25 to 0.25
- cap_mid: bfloat16 [4, 256, 512], replicated, may hold values from -0.25 to 0.25
- cap_low: bfloat16 [8, 256, 512], P('leaf'), may hold values from -0.25 to 0.25
Outputs:
- solution: float32 [64, 196608], P(None, ('leaf', 'rows'))
All inputs are finite; a program needn't handle non-finite values.
Results may differ from a plain program's by a relative error of at most 0.019.
Values may be sent and summed in bfloat16 or wider, within the bound.
No kernel may reach another device: no remote copies, remote signals or barrier semaphores. Data moves between devices by JAX's collectives and lax.ppermute only.
A program may use at most 128 MiB of HBM per device.

v0:
```python
import jax
import jax.numpy as jnp
from jax import lax
from jax.sharding import PartitionSpec as P

NNZ = 3
LEVELS = 3


def tip_factor(tip_tags):
    return jnp.where(tip_tags == 1, 0.6, jnp.where(tip_tags == 2, 1.8, 1.0)).astype(jnp.float32)


def shards(
    right_side, tip_tags, leaf_blocks, leaf_cols, u_panels, v_panels, cap_top, cap_mid, cap_low
):
    width = right_side.shape[1]
    count_rows = lax.axis_size("rows")
    count_leaf = lax.axis_size("leaf")
    count_all = count_leaf * count_rows
    leaf_pos = lax.axis_index("leaf")
    global_pos = leaf_pos * count_rows + lax.axis_index("rows")
    scaled = (right_side * tip_factor(tip_tags)[None, :]).astype(jnp.bfloat16)
    columns = leaf_cols[0]
    field = jnp.dot(scaled, leaf_blocks[0], preferred_element_type=jnp.float32)
    gathered = lax.all_gather(scaled, "rows", axis=1, tiled=True)
    for slot in range(NNZ - 1):
        block = lax.dynamic_slice_in_dim(gathered, columns[slot] * width, width, 1)
        field = field + jnp.dot(block, leaf_blocks[slot + 1], preferred_element_type=jnp.float32)
    caps = (cap_top, cap_mid, cap_low)
    for height in range(LEVELS):
        count = 2 ** (height + 1)
        child = global_pos // (count_all // count)
        side = child % 2
        rounded = field.astype(jnp.bfloat16)
        partial_value = lax.dot_general(
            rounded, v_panels[height], (((1,), (1,)), ((), ())), preferred_element_type=jnp.float32
        )
        marks = (jnp.arange(count, dtype=jnp.int32) == child).astype(jnp.float32)
        slotted = lax.psum(marks[:, None, None] * partial_value[None], ("leaf", "rows"))
        upper = slotted[child - side + 1]
        lower = slotted[child - side]
        stacked = jnp.concatenate([upper.astype(jnp.bfloat16), lower.astype(jnp.bfloat16)], axis=1)
        if height == LEVELS - 1:
            cap_rows = caps[height][child - leaf_pos * (8 // count_leaf)]
        else:
            cap_rows = caps[height][child]
        mixed = lax.dot_general(
            stacked, cap_rows, (((1,), (1,)), ((), ())), preferred_element_type=jnp.float32
        ).astype(jnp.bfloat16)
        field = field - jnp.dot(mixed, u_panels[height], preferred_element_type=jnp.float32)
    return field


def solution(mesh):
    placed = (
        P(None, ("leaf", "rows")),
        P(("leaf", "rows")),
        P(None, None, ("leaf", "rows")),
        P(("leaf", "rows"), None),
        P(None, None, ("leaf", "rows")),
        P(None, None, ("leaf", "rows")),
        P(),
        P(),
        P("leaf", None, None),
    )
    return jax.shard_map(
        shards, mesh=mesh, in_specs=placed, out_specs=P(None, ("leaf", "rows")), check_vma=False
    )
```

profile of v0, /device:TPU:1, one launch (start us, length us, event | category | flops | bytes accessed | tf_op | source)
XLA Modules:
  0.0 402.6 jit_solution(16752718354547489303)
XLA Ops:
  6.5 0.0 copy-start
  6.5 0.0 copy-start.1
  6.5 0.0 copy-start.2
  6.5 0.0 all-gather.2.cloned.1.call-start
  6.5 0.8 select_select_fusion
  7.4 1.5 multiply_convert_fusion
  8.9 0.0 all-gather.2.cloned.1.call-update
  8.9 1.3 fusion.73
  11.7 1.2 fusion.2
  12.8 0.0 copy-start.3
  12.8 83.4 %all-gather.2.cloned.1.call-done = bf16[64,24576]{1,0:T(8,128)(2,1)} async-done(((bf16[64,384]{1,0:T(8,128)(2,1)}), bf16[64,24576]{1,0:T(8,128)(2,1)}) %all-gather.2.cloned.1.call-update) | async-done | bytes 3145744 | tf_op jit(solution)/shard_map/all_gather | solution.py:26
  96.2 1.2 convolution_add_fusion.1
  97.4 1.2 convolution_add_fusion
  98.6 1.1 fusion.24
  99.7 0.1 broadcast_multiply_fusion.2
  99.8 99.6 %all-reduce.3 = bf16[2,64,256]{2,1,0:T(8,128)(2,1)S(1)} all-reduce(f32[2,64,256]{2,1,0:T(8,128)S(1)} %broadcast_multiply_fusion.2), channel_id=1, replica_groups=mesh['leaf'=8,'rows'=64] {'leaf','rows'}, use_global_device_ids=true, to_apply=%region_0.1 | all-reduce | flops 32768 | bytes 196608 | tf_op jit(solution)/shard_map/psum | solution.py:40
  199.5 1.3 convolution_subtract_fusion.2
  200.8 0.0 copy-done.1
  200.8 0.2 fusion.21
  201.0 0.1 broadcast_multiply_fusion.1
  201.1 94.8 %all-reduce.4 = bf16[4,64,256]{2,1,0:T(8,128)(2,1)S(1)} all-reduce(f32[4,64,256]{2,1,0:T(8,128)S(1)} %broadcast_multiply_fusion.1), channel_id=1, replica_groups=mesh['leaf'=8,'rows'=64] {'leaf','rows'}, use_global_device_ids=true, to_apply=%region_1.2 | all-reduce | flops 65536 | bytes 393216 | tf_op jit(solution)/shard_map/psum | solution.py:40
  295.9 0.0 copy-done
  295.9 0.0 copy-done.2
  295.9 0.3 convolution_subtract_fusion.1
  296.2 0.2 fusion.18
  296.5 0.1 broadcast_multiply_fusion
  296.6 98.2 %all-reduce.5 = bf16[8,64,256]{2,1,0:T(8,128)(2,1)S(1)} all-reduce(f32[8,64,256]{2,1,0:T(8,128)S(1)} %broadcast_multiply_fusion), channel_id=1, replica_groups=mesh['leaf'=8,'rows'=64] {'leaf','rows'}, use_global_device_ids=true, to_apply=%region_2.3 | all-reduce | flops 131072 | bytes 786432 | tf_op jit(solution)/shard_map/psum | solution.py:40
  394.8 0.0 copy-done.3
  394.8 1.0 convolution_subtract_fusion
  (6 shorter events, 0.1 us)
Async XLA Ops:
  6.5 289.4 %copy-start = (bf16[4,256,512]{2,1,0:T(8,128)(2,1)S(1)}, bf16[4,256,512]{2,1,0:T(8,128)(2,1)}, u32[]{:S(2)}) copy-start(bf16[4,256,512]{2,1,0:T(8,128)(2,1)} %param.16) | copy-start | bytes 3145732
  6.5 194.3 %copy-start.1 = (bf16[3,256,384]{2,1,0:T(8,128)(2,1)S(1)}, bf16[3,256,384]{2,1,0:T(8,128)(2,1)}, u32[]{:S(2)}) copy-start(bf16[3,256,384]{2,1,0:T(8,128)(2,1)} %param.14) | copy-start | bytes 1769476
  6.5 289.4 %copy-start.2 = (bf16[3,256,384]{2,1,0:T(8,128)(2,1)S(1)}, bf16[3,256,384]{2,1,0:T(8,128)(2,1)}, u32[]{:S(2)}) copy-start(bf16[3,256,384]{2,1,0:T(8,128)(2,1)} %param.13) | copy-start | bytes 1769476
  6.5 89.7 %all-gather.2.cloned.1.call-start = ((), (), s32[]{:S(2)}) async-start(), calls=%async_computation | async-start | bytes 3194880 | tf_op jit(solution)/shard_map/all_gather | solution.py:26
  12.8 381.9 %copy-start.3 = (bf16[1,256,512]{2,1,0:T(8,128)(2,1)S(1)}, bf16[1,256,512]{2,1,0:T(8,128)(2,1)}, u32[]{:S(2)}) copy-start(bf16[1,256,512]{2,1,0:T(8,128)(2,1)} %param.17) | copy-start | bytes 786436
Sparse Core Ops, SparseCore 0:
  10.6 85.6 all-gather.1
where the time goes:
time: 403 us
  blocking collectives  293 us (73%)
  waiting for transfers between devices  83.4 us (21%)
  between operations  14.9 us (4%)
  matrix products  7.67 us (2%)
    psum x3, blocking collectives, shards(): lax.psum(marks[:, None, None] * partial_value[None], ('leaf', 'rows'))  293 us
    all_gather x1, waiting for transfers between devices, shards(): gathered = lax.all_gather(scaled, 'rows', axis=1, tiled=True)  83.4 us
  transfers between devices with their start and end apart: 1, of which 1 were waited for; matrix products, arithmetic and copies ran while one was open for 1% of the time, Pallas kernels for 0%

commit v1 on v0

v1 whole, which is shorter than its diff:
```python
import jax
import jax.numpy as jnp
from jax import lax
from jax.sharding import PartitionSpec as P

NNZ = 3
LEVELS = 3
LANES = 128


def tip_factor(tip_tags):
    return jnp.where(tip_tags == 1, 0.6, jnp.where(tip_tags == 2, 1.8, 1.0)).astype(jnp.float32)


def dot_nt(a, b):
    return lax.dot_general(a, b, (((1,), (1,)), ((), ())), preferred_element_type=jnp.float32)


def swap(value, step, count):
    return lax.ppermute(value, "leaf", [(i, i ^ step) for i in range(count)])


def exchange(value, axis):
    return lax.all_to_all(value, axis, 0, 0, tiled=True)


def shards(
    right_side, tip_tags, leaf_blocks, leaf_cols, u_panels, v_panels, cap_top, cap_mid, cap_low
):
    nrhs, width = right_side.shape
    rank = u_panels.shape[1]
    rows = lax.axis_size("rows")
    leaves = lax.axis_size("leaf")
    leaf_pos = lax.axis_index("leaf")
    share = rank // rows
    bf16 = jnp.bfloat16

    scaled = (right_side * tip_factor(tip_tags)[None, :]).astype(bf16)

    w_first = dot_nt(u_panels[0], v_panels[1:].reshape(2 * rank, width))
    w_second = dot_nt(u_panels[1], v_panels[2])
    w_part = jnp.concatenate([w_first, w_second], axis=1).astype(bf16).reshape(rows, share, 3 * rank)

    columns = jnp.pad(leaf_cols.astype(bf16), ((0, 0), (0, LANES - 2)))
    extra = jnp.concatenate(
        [
            scaled.reshape(rows, width // LANES, LANES),
            jnp.broadcast_to(columns[None], (rows, 1, LANES)),
        ],
        axis=1,
    )
    first = exchange(jnp.concatenate([w_part, extra], axis=2), "rows")
    w_sum = jnp.sum(first[:, :, : 3 * rank].astype(jnp.float32), axis=0)
    table = first[:, : width // LANES, 3 * rank :].reshape(rows, width)
    wanted = first[:, width // LANES, 3 * rank : 3 * rank + 2].astype(jnp.int32)

    hot = (wanted[:, :, None] == jnp.arange(rows, dtype=jnp.int32)).astype(bf16)
    picked = jnp.dot(hot.reshape(rows * 2, rows), table, preferred_element_type=jnp.float32).astype(bf16)
    second = exchange(picked.reshape(rows, 2, width), "rows")

    w_bf = w_sum.astype(bf16)
    w_other = swap(w_bf, 1, leaves)
    upper = (leaf_pos % 2) == 1
    pair = (w_sum[:, :rank] + w_other[:, :rank].astype(jnp.float32)).astype(bf16)
    pair_other = swap(pair, 2, leaves)
    pair_upper = ((leaf_pos // 2) % 2) == 1
    mid = lax.dynamic_index_in_dim(cap_mid, leaf_pos // 2, 0, keepdims=False)
    low = cap_low[0]
    top = lax.dynamic_index_in_dim(cap_top, leaf_pos // 4, 0, keepdims=False)

    def stack(mine, other, is_upper):
        return jnp.concatenate(
            [jnp.where(is_upper, mine, other), jnp.where(is_upper, other, mine)], axis=1
        )

    x_mid = dot_nt(stack(pair, pair_other, pair_upper), mid)
    later = stack(
        jnp.concatenate([w_bf[:, rank : 2 * rank], w_bf[:, 2 * rank :]], axis=0),
        jnp.concatenate([w_other[:, rank : 2 * rank], w_other[:, 2 * rank :]], axis=0),
        upper,
    )
    x_low = dot_nt(later, low)
    x_rows = jnp.concatenate([x_mid, x_low[:share], x_low[share:]], axis=1).astype(bf16)

    blocks = jnp.concatenate([scaled, second[:, 0], second[:, 1]], axis=1)
    field = jnp.dot(
        blocks, leaf_blocks.reshape(NNZ * width, width), preferred_element_type=jnp.float32
    )
    partial = dot_nt(field.astype(bf16), v_panels.reshape(LEVELS * rank, width)).astype(bf16)

    third = exchange(
        jnp.concatenate(
            [
                partial.reshape(rows, 2, 3 * rank // 2),
                jnp.broadcast_to(x_rows.reshape(1, 2, 6 * rank), (rows, 2, 6 * rank)),
            ],
            axis=2,
        ),
        "rows",
    )
    own = jnp.sum(third[:, :, : 3 * rank // 2].astype(jnp.float32), axis=0).reshape(1, 1, 3 * rank)
    x_all = third[:, :, 3 * rank // 2 :].reshape(rank, 3 * rank)

    every = exchange(jnp.broadcast_to(own, (leaves, 1, 3 * rank)), "leaf").reshape(leaves, LEVELS, rank)
    halves = every[:, 0].reshape(2, leaves // 2, rank).sum(axis=1)
    pairs = every[:, 1].reshape(leaves // 2, 2, rank).sum(axis=1)
    pairs = lax.dynamic_slice_in_dim(pairs, leaf_pos // 4 * 2, 2, 0)
    singles = lax.dynamic_slice_in_dim(every[:, 2], leaf_pos // 2 * 2, 2, 0)

    def coupled(both, cap):
        stacked = jnp.concatenate([both[1:2], both[0:1]], axis=1).astype(bf16)
        return dot_nt(stacked, cap)

    mixed_top = coupled(halves, top).astype(bf16)
    from_top = jnp.dot(mixed_top, x_all[:, : 2 * rank], preferred_element_type=jnp.float32)
    mixed_mid = (coupled(pairs, mid) - from_top[:, :rank]).astype(bf16)
    from_mid = jnp.dot(mixed_mid, x_all[:, 2 * rank :], preferred_element_type=jnp.float32)
    mixed_low = (coupled(singles, low) - from_top[:, rank:] - from_mid).astype(bf16)
    mixed = jnp.concatenate([mixed_top, mixed_mid, mixed_low], axis=1)

    last = exchange(jnp.broadcast_to(mixed[None], (rows, 1, 3 * rank)), "rows").reshape(nrhs, 3 * rank)
    return field - jnp.dot(
        last, u_panels.reshape(LEVELS * rank, width), preferred_element_type=jnp.float32
    )


def solution(mesh):
    placed = (
        P(None, ("leaf", "rows")),
        P(("leaf", "rows")),
        P(None, None, ("leaf", "rows")),
        P(("leaf", "rows"), None),
        P(None, None, ("leaf", "rows")),
        P(None, None, ("leaf", "rows")),
        P(),
        P(),
        P("leaf", None, None),
    )
    return jax.shard_map(
        shards, mesh=mesh, in_specs=placed, out_specs=P(None, ("leaf", "rows")), check_vma=False
    )
```

time: 403 us -> 119 us (0.30)
  blocking collectives: 293 us -> 42 us
  waiting for transfers between devices: 83.4 us -> 26.7 us
  starting transfers between devices: 0.01 us -> 35.2 us
  between operations: 14.9 us -> 0.5 us
  local copies, waits for them, and re-layouts: 1.38 us -> 8.46 us
  matrix products: 7.67 us -> 3.36 us
    psum x3 -> x0, blocking collectives: 293 us -> none  [shards(): lax.psum(marks[:, None, None] * partial_value[None], ('leaf', 'rows'))]
    all_gather x1 -> x0, waiting for transfers between devices: 83.4 us -> none  [shards(): gathered = lax.all_gather(scaled, 'rows', axis=1, tiled=True)]
    all_to_all x0 -> x2, blocking collectives: none -> 42 us  [exchange(): return lax.all_to_all(value, axis, 0, 0, tiled=True)]
    all_to_all x0 -> x3, waiting for transfers between devices: none -> 25.7 us  [exchange(): return lax.all_to_all(value, axis, 0, 0, tiled=True)]
    all_to_all x0 -> x3, starting transfers between devices: none -> 25.4 us  [exchange(): return lax.all_to_all(value, axis, 0, 0, tiled=True)]
    ppermute x0 -> x2, starting transfers between devices: none -> 9.8 us  [swap(): return lax.ppermute(value, 'leaf', [(i, i ^ step) for i in range(count)])]
    dot_general x9 -> x13, matrix products: 7.67 us -> 3.36 us  [the longest x8 1.7 us: dot_nt(): lax.dot_general(a, b, (((1,), (1,)), ((), ())), preferred_element_type=jn...]
  transfers between devices with their start and end apart: 1 -> 5, of which waited for: 1 -> 4; matrix products, arithmetic and copies ran while one was open for 1% -> 2% of each run, Pallas kernels for 0% -> 0%
where the time goes in v1:
time: 119 us
  blocking collectives  42 us (35%)
  starting transfers between devices  35.2 us (30%)
  waiting for transfers between devices  26.7 us (22%)
  local copies, waits for them, and re-layouts  8.46 us (7%)
  matrix products  3.36 us (3%)
  other arithmetic  2.34 us (2%)
    all_to_all x2, blocking collectives, exchange(): return lax.all_to_all(value, axis, 0, 0, tiled=True)  42 us
    all_to_all x3, waiting for transfers between devices, exchange(): return lax.all_to_all(value, axis, 0, 0, tiled=True)  25.7 us
    all_to_all x3, starting transfers between devices, exchange(): return lax.all_to_all(value, axis, 0, 0, tiled=True)  25.4 us
    ppermute x2, starting transfers between devices, swap(): return lax.ppermute(value, 'leaf', [(i, i ^ step) for i in range(count)])  9.8 us
    unnamed x20, local copies, waits for them, and re-layouts  2.75 us
  transfers between devices with their start and end apart: 5, of which 4 were waited for; matrix products, arithmetic and copies ran while one was open for 2% of the time, Pallas kernels for 0%

profile of v1, /device:TPU:1, one launch (start us, length us, event | category | flops | bytes accessed | tf_op | source)
XLA Modules:
  0.0 118.6 jit_solution(11055288147239751431)
XLA Ops:
  0.0 1.1 fusion.48
  1.2 0.1 dot_general.51
  1.3 1.0 copy-done.1
  2.3 0.3 convolution_convert_fusion.1
  2.5 0.4 copy-done.7
  3.0 0.6 copy-done.8
  3.7 0.3 convolution_convert_fusion
  4.0 0.5 copy-done.5
  4.6 0.1 maximum_maximum_fusion
  4.6 1.1 copy.59
  5.8 11.6 %all-to-all-start = ((bf16[64,4,896]{2,1,0:T(4,128)(2,1)}), bf16[64,4,896]{2,1,0:T(4,128)(2,1)S(1)}, u32[]{:S(2)}, u32[]{:S(2)}) async-start(bf16[64,4,896]{2,1,0:T(4,128)(2,1)} %copy.59), calls=%async_computation | async-start | bytes 917504 | tf_op jit(solution)/shard_map/all_to_all | solution.py:24
  17.5 16.3 %all-to-all-done = bf16[64,4,896]{2,1,0:T(4,128)(2,1)S(1)} async-done(((bf16[64,4,896]{2,1,0:T(4,128)(2,1)}), bf16[64,4,896]{2,1,0:T(4,128)(2,1)S(1)}, u32[]{:S(2)}, u32[]{:S(2)}) %all-to-all-start) | async-done | bytes 458784 | tf_op jit(solution)/shard_map/all_to_all | solution.py:24
  33.8 0.2 convert_reduce_fusion
  34.0 4.0 %collective-permute-start = (bf16[4,768]{1,0:T(4,128)(2,1)S(1)}, bf16[4,768]{1,0:T(4,128)(2,1)S(1)}, u32[]{:S(2)}, u32[]{:S(2)}) collective-permute-start(bf16[4,768]{1,0:T(4,128)(2,1)S(1)} %convert_element_type.85), channel_id=1, source_target_pairs={{0,64},{64,0},{128,192},{192,128},{256,320},{320,256},{384,448},{4... | collective-permute-start | bytes 18440 | tf_op jit(solution)/shard_map/ppermute | solution.py:20
  38.0 0.1 fusion.29
  38.1 0.1 reshape.138
  38.3 0.2 convolution_convert_fusion.3
  38.6 0.7 reshape.129
  39.2 5.9 %all-to-all-start.1 = ((bf16[64,2,384]{2,1,0:T(2,128)(2,1)}), bf16[64,2,384]{2,1,0:T(2,128)(2,1)S(1)}, u32[]{:S(2)}, u32[]{:S(2)}) async-start(bf16[64,2,384]{2,1,0:T(2,128)(2,1)} %reshape.129), calls=%async_computation.1 | async-start | bytes 196608 | tf_op jit(solution)/shard_map/all_to_all | solution.py:24
  45.2 5.8 %collective-permute-start.1 = (bf16[4,256]{1,0:T(4,128)(2,1)S(1)}, bf16[4,256]{1,0:T(4,128)(2,1)S(1)}, u32[]{:S(2)}, u32[]{:S(2)}) collective-permute-start(bf16[4,256]{1,0:T(4,128)(2,1)S(1)} %fusion.37), channel_id=1, source_target_pairs={{0,128},{64,192},{128,0},{192,64},{256,384},{320,448},{384,256},{4... | collective-permute-start | bytes 6152 | tf_op jit(solution)/shard_map/ppermute | solution.py:20
  51.1 0.1 convolution_convert_fusion.4
  51.2 1.1 collective-permute-done.1
  52.3 0.2 convolution_convert_fusion.5
  52.5 3.2 %all-to-all-done.1 = bf16[64,2,384]{2,1,0:T(2,128)(2,1)S(1)} async-done(((bf16[64,2,384]{2,1,0:T(2,128)(2,1)}), bf16[64,2,384]{2,1,0:T(2,128)(2,1)S(1)}, u32[]{:S(2)}, u32[]{:S(2)}) %all-to-all-start.1) | async-done | bytes 98336 | tf_op jit(solution)/shard_map/all_to_all | solution.py:24
  55.7 0.1 fusion.49
  55.9 0.3 fusion.17
  56.2 0.3 convolution_convert_fusion.2
  56.5 0.2 broadcast_in_dim.48
  56.8 0.4 pad_maximum_fusion
  57.2 24.5 %all_to_all.25 = bf16[64,2,1920]{2,1,0:T(2,128)(2,1)S(1)} all-to-all(bf16[64,2,1920]{2,1,0:T(2,128)(2,1)S(1)} %pad_maximum_fusion), channel_id=1, replica_groups=mesh['leaf'=8,'rows'=64] {'rows'}, dimensions={0} | all-to-all | bytes 983040 | tf_op jit(solution)/shard_map/all_to_all | solution.py:24
  81.7 0.1 slice.151
  81.8 0.6 broadcast_in_dim.50
  82.4 7.9 %all-to-all-start.3 = ((f32[8,1,768]{2,1,0:T(1,128)}), f32[8,1,768]{2,1,0:T(1,128)S(1)}, u32[]{:S(2)}, u32[]{:S(2)}) async-start(f32[8,1,768]{2,1,0:T(1,128)} %broadcast_in_dim.50), calls=%async_computation.3 | async-start | bytes 49152 | tf_op jit(solution)/shard_map/all_to_all | solution.py:24
  90.3 0.3 slice.158
  90.6 0.2 reshape.134
  90.8 6.1 %all-to-all-done.3 = f32[8,1,768]{2,1,0:T(1,128)S(1)} async-done(((f32[8,1,768]{2,1,0:T(1,128)}), f32[8,1,768]{2,1,0:T(1,128)S(1)}, u32[]{:S(2)}, u32[]{:S(2)}) %all-to-all-start.3) | async-done | bytes 24608 | tf_op jit(solution)/shard_map/all_to_all | solution.py:24
  97.0 0.1 reduce.1
  97.2 0.2 fusion.4
  97.6 0.1 fusion.2
  97.7 0.2 fusion
  97.9 0.2 convolution_subtract_fusion.1
  98.1 0.2 fusion.1
  98.3 0.1 broadcast_in_dim.52
  98.4 0.5 broadcast.34
  98.9 1.2 %reduce.23 = bf16[64,768]{1,0:T(8,128)(2,1)S(1)} reduce(bf16[64,1,768]{2,1,0:T(2,128)(2,1)S(1)} %broadcast_in_dim.52, bf16[]{:T(256)} %broadcast.34), dimensions={1}, to_apply=%broadcast_in_dim.52.reduce_sub_computation | reduce | bytes 196610 | tf_op jit(solution)/shard_map/broadcast_in_dim | solution.py:121
  100.2 17.5 %all_to_all.26 = bf16[64,2,384]{2,1,0:T(2,128)(2,1)S(1)} all-to-all(bf16[64,2,384]{2,1,0:T(2,128)(2,1)S(1)} %reshape.170), channel_id=1, replica_groups=mesh['leaf'=8,'rows'=64] {'rows'}, dimensions={0} | all-to-all | bytes 196608 | tf_op jit(solution)/shard_map/all_to_all | solution.py:24
  117.6 0.1 reshape.171
  117.7 0.9 convolution_subtract_fusion
  (60 shorter events, 0.7 us)
Async XLA Ops:
  0.0 52.3 %copy-start = (bf16[4,256,512]{2,1,0:T(8,128)(2,1)S(1)}, bf16[4,256,512]{2,1,0:T(8,128)(2,1)}, u32[]{:S(2)}) copy-start(bf16[4,256,512]{2,1,0:T(8,128)(2,1)} %param.16) | copy-start | bytes 3145732
  1.2 1.1 copy-start.1
  2.3 0.7 copy-start.7
  2.3 1.4 %slice-start = ((bf16[3,256,384]{2,1,0:T(8,128)(2,1)}), bf16[2,256,384]{2,1,0:T(8,128)(2,1)S(1)}, s32[]{:S(2)}) async-start(bf16[3,256,384]{2,1,0:T(8,128)(2,1)} %param.14), calls=%async_computation.5 | async-start | bytes 786432 | tf_op jit(solution)/shard_map/slice | solution.py:40
  3.0 0.7 copy-start.8
  3.6 0.9 copy-start.5
  5.8 28.0 %all-to-all-start = ((bf16[64,4,896]{2,1,0:T(4,128)(2,1)}), bf16[64,4,896]{2,1,0:T(4,128)(2,1)S(1)}, u32[]{:S(2)}, u32[]{:S(2)}) async-start(bf16[64,4,896]{2,1,0:T(4,128)(2,1)} %copy.59), calls=%async_computation | async-start | bytes 917504 | tf_op jit(solution)/shard_map/all_to_all | solution.py:24
  34.0 11.2 %collective-permute-start = (bf16[4,768]{1,0:T(4,128)(2,1)S(1)}, bf16[4,768]{1,0:T(4,128)(2,1)S(1)}, u32[]{:S(2)}, u32[]{:S(2)}) collective-permute-start(bf16[4,768]{1,0:T(4,128)(2,1)S(1)} %convert_element_type.85), channel_id=1, source_target_pairs={{0,64},{64,0},{128,192},{192,128},{256,320},{320,256},{384,448},{4... | collective-permute-start | bytes 18440 | tf_op jit(solution)/shard_map/ppermute | solution.py:20
  38.3 12.8 %copy-start.3 = (bf16[1,256,512]{2,1,0:T(8,128)(2,1)S(1)}, bf16[1,256,512]{2,1,0:T(8,128)(2,1)}, u32[]{:S(2)}) copy-start(bf16[1,256,512]{2,1,0:T(8,128)(2,1)} %param.17) | copy-start | bytes 786436
  38.5 17.4 %copy-start.4 = (bf16[3,384,384]{2,1,0:T(8,128)(2,1)S(1)}, bf16[3,384,384]{2,1,0:T(8,128)(2,1)}, u32[]{:S(2)}) copy-start(bf16[3,384,384]{2,1,0:T(8,128)(2,1)} %param.11) | copy-start | bytes 2654212
  39.2 16.5 %all-to-all-start.1 = ((bf16[64,2,384]{2,1,0:T(2,128)(2,1)}), bf16[64,2,384]{2,1,0:T(2,128)(2,1)S(1)}, u32[]{:S(2)}, u32[]{:S(2)}) async-start(bf16[64,2,384]{2,1,0:T(2,128)(2,1)} %reshape.129), calls=%async_computation.1 | async-start | bytes 196608 | tf_op jit(solution)/shard_map/all_to_all | solution.py:24
  45.2 7.1 %collective-permute-start.1 = (bf16[4,256]{1,0:T(4,128)(2,1)S(1)}, bf16[4,256]{1,0:T(4,128)(2,1)S(1)}, u32[]{:S(2)}, u32[]{:S(2)}) collective-permute-start(bf16[4,256]{1,0:T(4,128)(2,1)S(1)} %fusion.37), channel_id=1, source_target_pairs={{0,128},{64,192},{128,0},{192,64},{256,384},{320,448},{384,256},{4... | collective-permute-start | bytes 6152 | tf_op jit(solution)/shard_map/ppermute | solution.py:20
  82.4 14.5 %all-to-all-start.3 = ((f32[8,1,768]{2,1,0:T(1,128)}), f32[8,1,768]{2,1,0:T(1,128)S(1)}, u32[]{:S(2)}, u32[]{:S(2)}) async-start(f32[8,1,768]{2,1,0:T(1,128)} %broadcast_in_dim.50), calls=%async_computation.3 | async-start | bytes 49152 | tf_op jit(solution)/shard_map/all_to_all | solution.py:24
  90.6 6.6 %copy-start.6 = (bf16[2,256,512]{2,1,0:T(8,128)(2,1)S(1)}, bf16[2,256,512]{2,1,0:T(8,128)(2,1)}, u32[]{:S(2)}) copy-start(bf16[2,256,512]{2,1,0:T(8,128)(2,1)} %param.15) | copy-start | bytes 1572868
  98.3 19.4 %copy-start.2 = (bf16[3,256,384]{2,1,0:T(8,128)(2,1)S(1)}, bf16[3,256,384]{2,1,0:T(8,128)(2,1)}, u32[]{:S(2)}) copy-start(bf16[3,256,384]{2,1,0:T(8,128)(2,1)} %param.13) | copy-start | bytes 1769476

commit v2 on v1

--- a/solution.py
+++ b/solution.py
@@ -16,8 +16,8 @@
     return lax.dot_general(a, b, (((1,), (1,)), ((), ())), preferred_element_type=jnp.float32)
 
 
-def swap(value, step, count):
-    return lax.ppermute(value, "leaf", [(i, i ^ step) for i in range(count)])
+def swap(value, axis, step):
+    return lax.ppermute(value, axis, [(i, i ^ step) for i in range(lax.axis_size(axis))])
 
 
 def exchange(value, axis):
@@ -32,14 +32,17 @@
     rows = lax.axis_size("rows")
     leaves = lax.axis_size("leaf")
     leaf_pos = lax.axis_index("leaf")
+    core = lax.axis_index("rows") % 2
     share = rank // rows
+    half = share // 2
     bf16 = jnp.bfloat16
 
     scaled = (right_side * tip_factor(tip_tags)[None, :]).astype(bf16)
 
     w_first = dot_nt(u_panels[0], v_panels[1:].reshape(2 * rank, width))
     w_second = dot_nt(u_panels[1], v_panels[2])
-    w_part = jnp.concatenate([w_first, w_second], axis=1).astype(bf16).reshape(rows, share, 3 * rank)
+    w_part = jnp.concatenate([w_first, w_second], axis=1).astype(bf16)
+    w_part = w_part.reshape(2, rows, half, 3 * rank).swapaxes(0, 1).reshape(rows, share, 3 * rank)
 
     columns = jnp.pad(leaf_cols.astype(bf16), ((0, 0), (0, LANES - 2)))
     extra = jnp.concatenate(
@@ -58,11 +61,11 @@
     picked = jnp.dot(hot.reshape(rows * 2, rows), table, preferred_element_type=jnp.float32).astype(bf16)
     second = exchange(picked.reshape(rows, 2, width), "rows")
 
-    w_bf = w_sum.astype(bf16)
-    w_other = swap(w_bf, 1, leaves)
+    w_bf, picked = lax.optimization_barrier((w_sum.astype(bf16), picked))
+    w_other = swap(w_bf, "leaf", 1)
     upper = (leaf_pos % 2) == 1
     pair = (w_sum[:, :rank] + w_other[:, :rank].astype(jnp.float32)).astype(bf16)
-    pair_other = swap(pair, 2, leaves)
+    pair_other = swap(pair, "leaf", 2)
     pair_upper = ((leaf_pos // 2) % 2) == 1
     mid = lax.dynamic_index_in_dim(cap_mid, leaf_pos // 2, 0, keepdims=False)
     low = cap_low[0]
@@ -88,20 +91,23 @@
     )
     partial = dot_nt(field.astype(bf16), v_panels.reshape(LEVELS * rank, width)).astype(bf16)
 
+    x_half = jnp.broadcast_to(x_rows.reshape(1, 2, half, 3 * rank), (rows // 2, 2, half, 3 * rank))
     third = exchange(
         jnp.concatenate(
             [
-                partial.reshape(rows, 2, 3 * rank // 2),
-                jnp.broadcast_to(x_rows.reshape(1, 2, 6 * rank), (rows, 2, 6 * rank)),
+                partial.reshape(rows, half, 3 * rank // half),
+                x_half.reshape(rows, half, 3 * rank),
             ],
             axis=2,
         ),
         "rows",
     )
-    own = jnp.sum(third[:, :, : 3 * rank // 2].astype(jnp.float32), axis=0).reshape(1, 1, 3 * rank)
-    x_all = third[:, :, 3 * rank // 2 :].reshape(rank, 3 * rank)
+    own = jnp.sum(third[:, :, : 3 * rank // half].astype(jnp.float32), axis=0).astype(bf16)
+    x_mine = third[:, :, 3 * rank // half :].reshape(rank // 2, 3 * rank)
+    x_theirs = swap(x_mine, "rows", 1)
 
-    every = exchange(jnp.broadcast_to(own, (leaves, 1, 3 * rank)), "leaf").reshape(leaves, LEVELS, rank)
+    every = exchange(jnp.broadcast_to(own[None], (leaves,) + own.shape), "leaf")
+    every = every.reshape(leaves, LEVELS, rank).astype(jnp.float32)
     halves = every[:, 0].reshape(2, leaves // 2, rank).sum(axis=1)
     pairs = every[:, 1].reshape(leaves // 2, 2, rank).sum(axis=1)
     pairs = lax.dynamic_slice_in_dim(pairs, leaf_pos // 4 * 2, 2, 0)
@@ -111,14 +117,23 @@
         stacked = jnp.concatenate([both[1:2], both[0:1]], axis=1).astype(bf16)
         return dot_nt(stacked, cap)
 
+    def through(mixed, at):
+        lower, upper_half = mixed[:, : rank // 2], mixed[:, rank // 2 :]
+        mine = jnp.where(core == 1, upper_half, lower)
+        theirs = jnp.where(core == 1, lower, upper_half)
+        return jnp.dot(mine, x_mine[:, at], preferred_element_type=jnp.float32) + jnp.dot(
+            theirs, x_theirs[:, at], preferred_element_type=jnp.float32
+        )
+
     mixed_top = coupled(halves, top).astype(bf16)
-    from_top = jnp.dot(mixed_top, x_all[:, : 2 * rank], preferred_element_type=jnp.float32)
+    from_top = through(mixed_top, slice(0, 2 * rank))
     mixed_mid = (coupled(pairs, mid) - from_top[:, :rank]).astype(bf16)
-    from_mid = jnp.dot(mixed_mid, x_all[:, 2 * rank :], preferred_element_type=jnp.float32)
+    from_mid = through(mixed_mid, slice(2 * rank, 3 * rank))
     mixed_low = (coupled(singles, low) - from_top[:, rank:] - from_mid).astype(bf16)
     mixed = jnp.concatenate([mixed_top, mixed_mid, mixed_low], axis=1)
 
-    last = exchange(jnp.broadcast_to(mixed[None], (rows, 1, 3 * rank)), "rows").reshape(nrhs, 3 * rank)
+    mixed = mixed.reshape(1, 2, 3 * rank // 2)
+    last = exchange(jnp.broadcast_to(mixed, (rows,) + mixed.shape[1:]), "rows").reshape(nrhs, 3 * rank)
     return field - jnp.dot(
         last, u_panels.reshape(LEVELS * rank, width), preferred_element_type=jnp.float32
     )

time: 119 us -> 113 us (0.950)
  blocking collectives: 42 us -> 37.8 us
  starting transfers between devices: 35.2 us -> 37.7 us
  local copies, waits for them, and re-layouts: 8.46 us -> 6.16 us
  waiting for transfers between devices: 26.7 us -> 24.6 us
    all_to_all x2, blocking collectives: 42 us -> 37.8 us  [exchange(): return lax.all_to_all(value, axis, 0, 0, tiled=True)]
    ppermute x2 -> x3, starting transfers between devices: 9.8 us -> 12.3 us  [swap(): lax.ppermute(value, axis, [(i, i ^ step) for i in range(lax.axis_size(axi...]
    all_to_all x3, waiting for transfers between devices: 25.7 us -> 23.6 us  [exchange(): return lax.all_to_all(value, axis, 0, 0, tiled=True)]
    broadcast_in_dim x1 -> x0, other arithmetic: 1.2 us -> none  [shards(): jnp.broadcast_to(mixed[None], (rows, 1, 3 * rank))]
    unnamed x20 -> x19, local copies, waits for them, and re-layouts: 2.75 us -> 2.21 us
  transfers between devices with their start and end apart: 5 -> 6, of which waited for: 4 -> 4; matrix products, arithmetic and copies ran while one was open for 2% -> 2% of each run, Pallas kernels for 0% -> 0%
where the time goes in v2:
time: 113 us; the launch traced here: 112 us
  blocking collectives  37.8 us (33%)
  starting transfers between devices  37.7 us (33%)
  waiting for transfers between devices  24.6 us (22%)
  local copies, waits for them, and re-layouts  6.16 us (5%)
  matrix products  3.57 us (3%)
  other arithmetic  2 us (2%)
    all_to_all x2, blocking collectives, exchange(): return lax.all_to_all(value, axis, 0, 0, tiled=True)  37.8 us
    all_to_all x3, starting transfers between devices, exchange(): return lax.all_to_all(value, axis, 0, 0, tiled=True)  25.4 us
    all_to_all x3, waiting for transfers between devices, exchange(): return lax.all_to_all(value, axis, 0, 0, tiled=True)  23.6 us
    ppermute x3, starting transfers between devices, swap(): lax.ppermute(value, axis, [(i, i ^ step) for i in range(lax.axis_size(axi...  12.3 us
  transfers between devices with their start and end apart: 6, of which 4 were waited for; matrix products, arithmetic and copies ran while one was open for 2% of the time, Pallas kernels for 0%

profile of v2, /device:TPU:1, one launch (start us, length us, event | category | flops | bytes accessed | tf_op | source)
XLA Modules:
  0.0 112.3 jit_solution(17237872321074511397)
XLA Ops:
  0.0 1.1 %fusion.63 = (bf16[1,256,384]{2,1,0:T(8,128)(2,1)S(1)}, bf16[1,256,384]{2,1,0:T(8,128)(2,1)S(1)}) fusion(bf16[3,256,384]{2,1,0:T(8,128)(2,1)} %param.13), kind=kLoop, calls=%fused_computation.108 | loop fusion | bytes 786432 | tf_op jit(solution)/shard_map/slice | solution.py:42
  1.2 0.1 dot_general.53
  1.3 0.1 dot_general.55
  1.3 1.0 copy-done.1
  2.3 0.3 convolution_convert_fusion.1
  2.6 0.3 convolution_convert_fusion
  3.0 0.3 copy.34
  3.3 0.3 copy-done.7
  3.6 0.2 copy-done.6
  3.9 0.6 copy-done.8
  4.5 1.0 maximum_maximum_fusion
  5.6 11.6 %all-to-all-start = ((bf16[64,4,896]{2,1,0:T(4,128)(2,1)}), bf16[64,4,896]{2,1,0:T(4,128)(2,1)S(1)}, u32[]{:S(2)}, u32[]{:S(2)}) async-start(bf16[64,4,896]{2,1,0:T(4,128)(2,1)} %maximum_maximum_fusion), calls=%async_computation | async-start | bytes 917504 | tf_op jit(solution)/shard_map/all_to_all | solution.py:24
  17.2 16.3 %all-to-all-done = bf16[64,4,896]{2,1,0:T(4,128)(2,1)S(1)} async-done(((bf16[64,4,896]{2,1,0:T(4,128)(2,1)}), bf16[64,4,896]{2,1,0:T(4,128)(2,1)S(1)}, u32[]{:S(2)}, u32[]{:S(2)}) %all-to-all-start) | async-done | bytes 458784 | tf_op jit(solution)/shard_map/all_to_all | solution.py:24
  33.6 0.1 fusion.33
  33.7 0.1 reshape.180
  33.9 0.2 convert_reduce_fusion
  34.1 0.2 convolution_convert_fusion.3
  34.3 4.1 %collective-permute-start = (bf16[4,768]{1,0:T(4,128)(2,1)S(1)}, bf16[4,768]{1,0:T(4,128)(2,1)S(1)}, u32[]{:S(2)}, u32[]{:S(2)}) collective-permute-start(bf16[4,768]{1,0:T(4,128)(2,1)S(1)} %convert_element_type.87), channel_id=1, source_target_pairs={{0,64},{64,0},{128,192},{192,128},{256,320},{320,256},{384,448},{4... | collective-permute-start | bytes 18440 | tf_op jit(solution)/shard_map/ppermute | solution.py:20
  38.5 0.7 reshape.167
  39.2 5.9 %all-to-all-start.1 = ((bf16[64,2,384]{2,1,0:T(2,128)(2,1)}), bf16[64,2,384]{2,1,0:T(2,128)(2,1)S(1)}, u32[]{:S(2)}, u32[]{:S(2)}) async-start(bf16[64,2,384]{2,1,0:T(2,128)(2,1)} %reshape.167), calls=%async_computation.1 | async-start | bytes 196608 | tf_op jit(solution)/shard_map/all_to_all | solution.py:24
  45.1 5.8 %collective-permute-start.1 = (bf16[4,256]{1,0:T(4,128)(2,1)S(1)}, bf16[4,256]{1,0:T(4,128)(2,1)S(1)}, u32[]{:S(2)}, u32[]{:S(2)}) collective-permute-start(bf16[4,256]{1,0:T(4,128)(2,1)S(1)} %fusion.41), channel_id=1, source_target_pairs={{0,128},{64,192},{128,0},{192,64},{256,384},{320,448},{384,256},{4... | collective-permute-start | bytes 6152 | tf_op jit(solution)/shard_map/ppermute | solution.py:20
  51.0 0.1 convolution_convert_fusion.4
  51.2 1.0 collective-permute-done.1
  52.2 0.2 convolution_convert_fusion.5
  52.5 3.2 %all-to-all-done.1 = bf16[64,2,384]{2,1,0:T(2,128)(2,1)S(1)} async-done(((bf16[64,2,384]{2,1,0:T(2,128)(2,1)}), bf16[64,2,384]{2,1,0:T(2,128)(2,1)S(1)}, u32[]{:S(2)}, u32[]{:S(2)}) %all-to-all-start.1) | async-done | bytes 98336 | tf_op jit(solution)/shard_map/all_to_all | solution.py:24
  55.7 0.1 fusion.64
  55.8 0.3 fusion.16
  56.1 0.3 convolution_convert_fusion.2
  56.5 0.1 broadcast_in_dim.46
  56.6 0.3 pad_maximum_fusion.1
  56.8 21.2 %all_to_all.25 = bf16[64,2,1152]{2,1,0:T(2,128)(2,1)S(1)} all-to-all(bf16[64,2,1152]{2,1,0:T(2,128)(2,1)S(1)} %pad_maximum_fusion.1), channel_id=1, replica_groups=mesh['leaf'=8,'rows'=64] {'rows'}, dimensions={0} | all-to-all | bytes 589824 | tf_op jit(solution)/shard_map/all_to_all | solution.py:24
  78.0 0.1 slice_reduce_fusion
  78.2 0.6 broadcast_in_dim.47
  78.8 7.9 %all-to-all-start.3 = ((bf16[8,2,384]{2,1,0:T(2,128)(2,1)}), bf16[8,2,384]{2,1,0:T(2,128)(2,1)S(1)}, u32[]{:S(2)}, u32[]{:S(2)}) async-start(bf16[8,2,384]{2,1,0:T(2,128)(2,1)} %broadcast_in_dim.47), calls=%async_computation.3 | async-start | bytes 24576 | tf_op jit(solution)/shard_map/all_to_all | solution.py:24
  86.6 0.1 slice.182
  86.8 0.1 reshape.174
  86.9 2.3 %collective-permute-start.2 = (bf16[128,768]{1,0:T(8,128)(2,1)S(1)}, bf16[128,768]{1,0:T(8,128)(2,1)S(1)}, u32[]{:S(2)}, u32[]{:S(2)}) collective-permute-start(bf16[128,768]{1,0:T(8,128)(2,1)S(1)} %reshape.174), channel_id=1, source_target_pairs={{0,1},{1,0},{2,3},{3,2},{4,5},{5,4},{6,7},{7,6},{8,9},{9,8},{10,11... | collective-permute-start | bytes 589832 | tf_op jit(solution)/shard_map/ppermute | solution.py:20
  89.2 4.1 %all-to-all-done.3 = bf16[8,2,384]{2,1,0:T(2,128)(2,1)S(1)} async-done(((bf16[8,2,384]{2,1,0:T(2,128)(2,1)}), bf16[8,2,384]{2,1,0:T(2,128)(2,1)S(1)}, u32[]{:S(2)}, u32[]{:S(2)}) %all-to-all-start.3) | async-done | bytes 12320 | tf_op jit(solution)/shard_map/all_to_all | solution.py:24
  93.5 0.2 fusion.3
  93.8 0.1 fusion.24
  93.9 0.1 fusion.22
  94.1 0.2 fusion
  94.2 0.2 fusion.28
  94.4 0.1 fusion.26
  94.5 0.2 fusion.2
  94.8 0.1 broadcast_in_dim.49
  94.8 16.6 %all_to_all.26 = bf16[64,2,384]{2,1,0:T(2,128)(2,1)S(1)} all-to-all(bf16[64,2,384]{2,1,0:T(2,128)(2,1)S(1)} %broadcast_in_dim.49), channel_id=1, replica_groups=mesh['leaf'=8,'rows'=64] {'rows'}, dimensions={0} | all-to-all | bytes 196608 | tf_op jit(solution)/shard_map/all_to_all | solution.py:24
  111.5 0.9 convolution_subtract_fusion
  (64 shorter events, 0.8 us)
Async XLA Ops:
  0.0 52.2 %copy-start = (bf16[4,256,512]{2,1,0:T(8,128)(2,1)S(1)}, bf16[4,256,512]{2,1,0:T(8,128)(2,1)}, u32[]{:S(2)}) copy-start(bf16[4,256,512]{2,1,0:T(8,128)(2,1)} %param.16) | copy-start | bytes 3145732
  1.2 1.1 copy-start.1
  1.3 1.3 %slice-start = ((bf16[3,256,384]{2,1,0:T(8,128)(2,1)}), bf16[2,256,384]{2,1,0:T(8,128)(2,1)S(1)}, s32[]{:S(2)}) async-start(bf16[3,256,384]{2,1,0:T(8,128)(2,1)} %param.14), calls=%async_computation.5 | async-start | bytes 786432 | tf_op jit(solution)/shard_map/slice | solution.py:42
  2.9 0.7 copy-start.7
  3.0 0.9 copy-start.6
  3.9 0.7 copy-start.8
  5.6 28.0 %all-to-all-start = ((bf16[64,4,896]{2,1,0:T(4,128)(2,1)}), bf16[64,4,896]{2,1,0:T(4,128)(2,1)S(1)}, u32[]{:S(2)}, u32[]{:S(2)}) async-start(bf16[64,4,896]{2,1,0:T(4,128)(2,1)} %maximum_maximum_fusion), calls=%async_computation | async-start | bytes 917504 | tf_op jit(solution)/shard_map/all_to_all | solution.py:24
  34.1 16.9 %copy-start.3 = (bf16[1,256,512]{2,1,0:T(8,128)(2,1)S(1)}, bf16[1,256,512]{2,1,0:T(8,128)(2,1)}, u32[]{:S(2)}) copy-start(bf16[1,256,512]{2,1,0:T(8,128)(2,1)} %param.17) | copy-start | bytes 786436
  34.3 21.5 %copy-start.4 = (bf16[3,384,384]{2,1,0:T(8,128)(2,1)S(1)}, bf16[3,384,384]{2,1,0:T(8,128)(2,1)}, u32[]{:S(2)}) copy-start(bf16[3,384,384]{2,1,0:T(8,128)(2,1)} %param.11) | copy-start | bytes 2654212
  34.3 10.8 %collective-permute-start = (bf16[4,768]{1,0:T(4,128)(2,1)S(1)}, bf16[4,768]{1,0:T(4,128)(2,1)S(1)}, u32[]{:S(2)}, u32[]{:S(2)}) collective-permute-start(bf16[4,768]{1,0:T(4,128)(2,1)S(1)} %convert_element_type.87), channel_id=1, source_target_pairs={{0,64},{64,0},{128,192},{192,128},{256,320},{320,256},{384,448},{4... | collective-permute-start | bytes 18440 | tf_op jit(solution)/shard_map/ppermute | solution.py:20
  39.2 16.5 %all-to-all-start.1 = ((bf16[64,2,384]{2,1,0:T(2,128)(2,1)}), bf16[64,2,384]{2,1,0:T(2,128)(2,1)S(1)}, u32[]{:S(2)}, u32[]{:S(2)}) async-start(bf16[64,2,384]{2,1,0:T(2,128)(2,1)} %reshape.167), calls=%async_computation.1 | async-start | bytes 196608 | tf_op jit(solution)/shard_map/all_to_all | solution.py:24
  45.1 7.1 %collective-permute-start.1 = (bf16[4,256]{1,0:T(4,128)(2,1)S(1)}, bf16[4,256]{1,0:T(4,128)(2,1)S(1)}, u32[]{:S(2)}, u32[]{:S(2)}) collective-permute-start(bf16[4,256]{1,0:T(4,128)(2,1)S(1)} %fusion.41), channel_id=1, source_target_pairs={{0,128},{64,192},{128,0},{192,64},{256,384},{320,448},{384,256},{4... | collective-permute-start | bytes 6152 | tf_op jit(solution)/shard_map/ppermute | solution.py:20
  78.2 15.3 %copy-start.5 = (bf16[2,256,512]{2,1,0:T(8,128)(2,1)S(1)}, bf16[2,256,512]{2,1,0:T(8,128)(2,1)}, u32[]{:S(2)}) copy-start(bf16[2,256,512]{2,1,0:T(8,128)(2,1)} %param.15) | copy-start | bytes 1572868
  78.8 14.5 %all-to-all-start.3 = ((bf16[8,2,384]{2,1,0:T(2,128)(2,1)}), bf16[8,2,384]{2,1,0:T(2,128)(2,1)S(1)}, u32[]{:S(2)}, u32[]{:S(2)}) async-start(bf16[8,2,384]{2,1,0:T(2,128)(2,1)} %broadcast_in_dim.47), calls=%async_computation.3 | async-start | bytes 24576 | tf_op jit(solution)/shard_map/all_to_all | solution.py:24
  86.9 7.1 %collective-permute-start.2 = (bf16[128,768]{1,0:T(8,128)(2,1)S(1)}, bf16[128,768]{1,0:T(8,128)(2,1)S(1)}, u32[]{:S(2)}, u32[]{:S(2)}) collective-permute-start(bf16[128,768]{1,0:T(8,128)(2,1)S(1)} %reshape.174), channel_id=1, source_target_pairs={{0,1},{1,0},{2,3},{3,2},{4,5},{5,4},{6,7},{7,6},{8,9},{9,8},{10,11... | collective-permute-start | bytes 589832 | tf_op jit(solution)/shard_map/ppermute | solution.py:20
  94.1 17.4 %copy-start.2 = (bf16[3,256,384]{2,1,0:T(8,128)(2,1)S(1)}, bf16[3,256,384]{2,1,0:T(8,128)(2,1)}, u32[]{:S(2)}) copy-start(bf16[3,256,384]{2,1,0:T(8,128)(2,1)} %param.13) | copy-start | bytes 1769476

commit v3 on v1

v3 whole, which is shorter than its diff:
```python
import jax
import jax.numpy as jnp
from jax import lax
from jax.sharding import PartitionSpec as P

NNZ = 3
LEVELS = 3
LANES = 128
CORES = 2


def tip_factor(tip_tags):
    return jnp.where(tip_tags == 1, 0.6, jnp.where(tip_tags == 2, 1.8, 1.0)).astype(jnp.float32)


def dot(a, b):
    return jnp.dot(a, b, preferred_element_type=jnp.float32)


def dot_nt(a, b):
    return lax.dot_general(a, b, (((1,), (1,)), ((), ())), preferred_element_type=jnp.float32)


def swap_cores(value):
    return lax.ppermute(value, "rows", [(i, i ^ 1) for i in range(lax.axis_size("rows"))])


def exchange(value, axis):
    return lax.all_to_all(value, axis, 0, 0, tiled=True)


def shards(
    right_side, tip_tags, leaf_blocks, leaf_cols, u_panels, v_panels, cap_top, cap_mid, cap_low
):
    nrhs, width = right_side.shape
    rank = u_panels.shape[1]
    half = rank // CORES
    wide = LEVELS * rank
    rows = lax.axis_size("rows")
    leaves = lax.axis_size("leaf")
    leaf_pos = lax.axis_index("leaf")
    second_core = lax.axis_index("rows") % CORES == 1
    bf16 = jnp.bfloat16

    def mine_theirs(lower, upper):
        return jnp.where(second_core, upper, lower), jnp.where(second_core, lower, upper)

    scaled = (right_side * tip_factor(tip_tags)[None, :]).astype(bf16)

    columns = jnp.pad(leaf_cols.astype(bf16), ((0, 0), (0, LANES - 2)))
    own_rows = jnp.concatenate(
        [
            scaled.reshape(rows, width // LANES, LANES),
            jnp.broadcast_to(columns[None], (rows, 1, LANES)),
        ],
        axis=1,
    )
    first = exchange(own_rows, "rows")
    table = first[:, : width // LANES].reshape(rows, width)
    wanted = first[:, width // LANES, :2].astype(jnp.int32)

    u_here, v_here, _ = lax.optimization_barrier((u_panels, v_panels, own_rows))
    w_first = dot_nt(u_here[0], v_here[1:].reshape(2 * rank, width))
    w_second = dot_nt(u_here[1], v_here[2])
    w_all = jnp.concatenate([w_first, w_second], axis=1).astype(bf16)
    w_mine, w_theirs = mine_theirs(w_all[:half], w_all[half:])
    w_chip = (w_mine.astype(jnp.float32) + swap_cores(w_theirs).astype(jnp.float32)).astype(bf16)

    hot = (wanted[:, :, None] == jnp.arange(rows, dtype=jnp.int32)).astype(bf16)
    picked = dot(hot.reshape(rows * 2, rows), table).astype(bf16)
    second = exchange(picked.reshape(rows, 2, width), "rows")

    blocks = jnp.concatenate([scaled, second[:, 0], second[:, 1]], axis=1)
    field = dot(blocks, leaf_blocks.reshape(NNZ * width, width))
    partial = dot_nt(field.astype(bf16), v_panels.reshape(wide, width)).astype(bf16)

    third = exchange(
        jnp.concatenate(
            [partial.reshape(rows, 2, wide // 2), w_chip.reshape(rows, half // rows, wide)], axis=2
        ),
        "rows",
    )
    third = third.reshape(rows // CORES, CORES, 2, 3 * wide // 2).astype(jnp.float32).sum(axis=0)
    own = third[:, :, : wide // 2].sum(axis=0)
    w_rows = third[:, :, wide // 2 :].reshape(CORES, 2 * wide)

    fourth = exchange(
        jnp.broadcast_to(
            jnp.concatenate([own, w_rows], axis=1).astype(bf16)[None], (leaves, 2, 5 * wide // 2)
        ),
        "leaf",
    ).astype(jnp.float32)
    every = fourth[:, :, : wide // 2].reshape(leaves, LEVELS, rank)
    w_every = fourth[:, :, wide // 2 :].reshape(leaves, 4, wide)

    def two_of(value, first_one):
        return lax.dynamic_slice_in_dim(value, first_one, 2, 0)

    def coupled(both, cap):
        return dot_nt(jnp.concatenate([both[1], both[0]], axis=1).astype(bf16), cap)

    top = lax.dynamic_index_in_dim(cap_top, leaf_pos // 4, 0, keepdims=False)
    mid = lax.dynamic_index_in_dim(cap_mid, leaf_pos // 2, 0, keepdims=False)
    low = cap_low[0]
    halves = every[:, 0].reshape(2, leaves // 2, 1, rank).sum(axis=1)
    mid_in = jnp.concatenate([every[:, 1:2], w_every[:, :, :rank]], axis=1)
    mid_in = two_of(mid_in.reshape(leaves // 2, 2, 5, rank).sum(axis=1), leaf_pos // 4 * 2)
    low_in = jnp.concatenate(
        [every[:, 2:3], w_every[:, :, rank : 2 * rank], w_every[:, :, 2 * rank :]], axis=1
    )
    low_in = two_of(low_in, leaf_pos // 2 * 2)
    top_out = coupled(halves, top)
    mid_out = coupled(mid_in, mid)
    low_out = coupled(low_in, low)
    start = jnp.concatenate([top_out, mid_out[:1], low_out[:1]], axis=1).astype(bf16)
    x_rows = jnp.concatenate([mid_out[1:], low_out[1:5], low_out[5:]], axis=1).astype(bf16)

    x_half = jnp.broadcast_to(x_rows.reshape(1, CORES, 2, wide), (rows // CORES, CORES, 2, wide))
    fifth = exchange(
        jnp.concatenate(
            [
                jnp.broadcast_to(start.reshape(1, 2, wide // 2), (rows, 2, wide // 2)),
                x_half.reshape(rows, 2, wide),
            ],
            axis=2,
        ),
        "rows",
    )
    x_mine = fifth[:, :, wide // 2 :].reshape(half, wide)
    x_theirs = swap_cores(x_mine)
    start = fifth[:, :, : wide // 2].reshape(nrhs, wide)
    mixed_top = start[:, :rank]

    def through(mixed, at):
        mine, theirs = mine_theirs(mixed[:, :half], mixed[:, half:])
        return dot(mine, x_mine[:, at]) + dot(theirs, x_theirs[:, at])

    from_top = through(mixed_top, slice(0, 2 * rank))
    mixed_mid = (start[:, rank : 2 * rank].astype(jnp.float32) - from_top[:, :rank]).astype(bf16)
    from_mid = through(mixed_mid, slice(2 * rank, wide))
    mixed_low = (start[:, 2 * rank :].astype(jnp.float32) - from_top[:, rank:] - from_mid).astype(bf16)
    mixed = jnp.concatenate([mixed_top, mixed_mid, mixed_low], axis=1)
    return field - dot(mixed, u_panels.reshape(wide, width))


def solution(mesh):
    placed = (
        P(None, ("leaf", "rows")),
        P(("leaf", "rows")),
        P(None, None, ("leaf", "rows")),
        P(("leaf", "rows"), None),
        P(None, None, ("leaf", "rows")),
        P(None, None, ("leaf", "rows")),
        P(),
        P(),
        P("leaf", None, None),
    )
    return jax.shard_map(
        shards, mesh=mesh, in_specs=placed, out_specs=P(None, ("leaf", "rows")), check_vma=False
    )
```

time: 119 us -> 106 us (0.89)
  blocking collectives: 42 us -> 37.3 us
  starting transfers between devices: 35.2 us -> 30.5 us
  local copies, waits for them, and re-layouts: 8.46 us -> 4.5 us
  waiting for transfers between devices: 26.7 us -> 24.7 us
  other arithmetic: 2.34 us -> 3.54 us
    ppermute x2, starting transfers between devices: 9.8 us -> 4.4 us  [swap_cores(): lax.ppermute(value, 'rows', [(i, i ^ 1) for i in range(lax.axis_size('row...]
    all_to_all x2, blocking collectives: 42 us -> 37.3 us  [exchange(): return lax.all_to_all(value, axis, 0, 0, tiled=True)]
    all_to_all x3, waiting for transfers between devices: 25.7 us -> 23.6 us  [exchange(): return lax.all_to_all(value, axis, 0, 0, tiled=True)]
    unnamed x20 -> x15, local copies, waits for them, and re-layouts: 2.75 us -> 0.69 us
    dot_general x5 -> x7, matrix products: 1.66 us -> 3.1 us  [dot(): return jnp.dot(a, b, preferred_element_type=jnp.float32)]
    broadcast_in_dim x1 -> x0, other arithmetic: 1.2 us -> none  [shards(): jnp.broadcast_to(mixed[None], (rows, 1, 3 * rank))]
where the time goes in v3:
time: 106 us; the launch traced here: 105 us
  blocking collectives  37.3 us (35%)
  starting transfers between devices  30.5 us (29%)
  waiting for transfers between devices  24.7 us (23%)
  local copies, waits for them, and re-layouts  4.5 us (4%)
  matrix products  4.46 us (4%)
  other arithmetic  3.54 us (3%)
    all_to_all x2, blocking collectives, exchange(): return lax.all_to_all(value, axis, 0, 0, tiled=True)  37.3 us
    all_to_all x3, starting transfers between devices, exchange(): return lax.all_to_all(value, axis, 0, 0, tiled=True)  26.1 us
    all_to_all x3, waiting for transfers between devices, exchange(): return lax.all_to_all(value, axis, 0, 0, tiled=True)  23.6 us
    ppermute x2, starting transfers between devices, swap_cores(): lax.ppermute(value, 'rows', [(i, i ^ 1) for i in range(lax.axis_size('row...  4.4 us
    dot_general x7, matrix products, dot(): return jnp.dot(a, b, preferred_element_type=jnp.float32)  3.1 us
  transfers between devices with their start and end apart: 5, of which 4 were waited for; matrix products, arithmetic and copies ran while one was open for 2% of the time, Pallas kernels for 0%

profile of v3, /device:TPU:1, one launch (start us, length us, event | category | flops | bytes accessed | tf_op | source)
XLA Modules:
  0.0 105.5 jit_solution(14490004958352493319)
XLA Ops:
  0.0 0.8 convert_element_type.86
  0.8 0.9 multiply_convert_fusion
  1.7 0.0 copy-start.2
  1.8 0.7 pad_maximum_fusion.3
  2.5 11.6 %all-to-all-start = ((bf16[64,4,128]{2,1,0:T(4,128)(2,1)}), bf16[64,4,128]{2,1,0:T(4,128)(2,1)S(1)}, u32[]{:S(2)}, u32[]{:S(2)}) async-start(bf16[64,4,128]{2,1,0:T(4,128)(2,1)} %pad_maximum_fusion.3), calls=%async_computation | async-start | bytes 131072 | tf_op jit(solution)/shard_map/all_to_all | solution.py:29
  14.1 0.0 slice-start
  14.1 1.1 %slice-done = bf16[2,256,384]{2,1,0:T(8,128)(2,1)S(1)} async-done(((bf16[3,256,384]{2,1,0:T(8,128)(2,1)}), bf16[2,256,384]{2,1,0:T(8,128)(2,1)S(1)}, s32[]{:S(2)}) %slice-start) | async-done | bytes 393240 | tf_op jit(solution)/shard_map/slice | solution.py:63
  15.3 0.3 convolution_convert_fusion
  15.6 0.3 convolution_convert_fusion.1
  15.9 2.4 %collective-permute-start = (bf16[128,768]{1,0:T(8,128)(2,1)S(1)}, bf16[128,768]{1,0:T(8,128)(2,1)S(1)}, u32[]{:S(2)}, u32[]{:S(2)}) collective-permute-start(bf16[128,768]{1,0:T(8,128)(2,1)S(1)} %broadcast_select_fusion), channel_id=1, source_target_pairs={{0,1},{1,0},{2,3},{3,2},{4,5},{5,4},{6,7},{7,6},{8,9},{9,8},{10,11... | collective-permute-start | bytes 589832 | tf_op jit(solution)/shard_map/ppermute | solution.py:25
  18.3 5.9 %all-to-all-done = bf16[64,4,128]{2,1,0:T(4,128)(2,1)S(1)} async-done(((bf16[64,4,128]{2,1,0:T(4,128)(2,1)}), bf16[64,4,128]{2,1,0:T(4,128)(2,1)S(1)}, u32[]{:S(2)}, u32[]{:S(2)}) %all-to-all-start) | async-done | bytes 65568 | tf_op jit(solution)/shard_map/all_to_all | solution.py:29
  24.2 0.1 fusion.39
  24.3 0.1 reshape.162
  24.4 0.2 convolution_convert_fusion.3
  24.7 0.7 reshape.149
  25.4 4.4 %all-to-all-start.1 = ((bf16[64,2,384]{2,1,0:T(2,128)(2,1)}), bf16[64,2,384]{2,1,0:T(2,128)(2,1)S(1)}, u32[]{:S(2)}, u32[]{:S(2)}) async-start(bf16[64,2,384]{2,1,0:T(2,128)(2,1)} %reshape.149), calls=%async_computation.1 | async-start | bytes 196608 | tf_op jit(solution)/shard_map/all_to_all | solution.py:29
  29.8 0.1 add_convert_fusion
  29.9 0.1 reshape.154
  30.0 10.5 %all-to-all-done.1 = bf16[64,2,384]{2,1,0:T(2,128)(2,1)S(1)} async-done(((bf16[64,2,384]{2,1,0:T(2,128)(2,1)}), bf16[64,2,384]{2,1,0:T(2,128)(2,1)S(1)}, u32[]{:S(2)}, u32[]{:S(2)}) %all-to-all-start.1) | async-done | bytes 98336 | tf_op jit(solution)/shard_map/all_to_all | solution.py:29
  40.5 0.1 fusion.75
  40.7 1.4 %fusion.13 = f32[64,384]{1,0:T(8,128)S(1)} fusion(bf16[1152,384]{1,0:T(8,128)(2,1)} %bitcast.61, bf16[64,384]{1,0:T(8,128)(2,1)S(1)} %get-tuple-element.23, bf16[64,384]{1,0:T(8,128)(2,1)S(1)} %get-tuple-element.24, bf16[64,384]{1,0:T(8,128)(2,1)S(1)} %multiply_convert_fusion), kind=kOutput, calls=%fused_computation.30 | convolution fusion | flops 57065472 | bytes 1130496 | tf_op jit(solution)/shard_map/dot_general | solution.py:17
  42.1 0.3 convolution_convert_fusion.2
  42.5 0.3 pad_maximum_fusion
  42.8 17.4 %all_to_all.25 = bf16[64,2,1152]{2,1,0:T(2,128)(2,1)S(1)} all-to-all(bf16[64,2,1152]{2,1,0:T(2,128)(2,1)S(1)} %pad_maximum_fusion), channel_id=1, replica_groups=mesh['leaf'=8,'rows'=64] {'rows'}, dimensions={0} | all-to-all | bytes 589824 | tf_op jit(solution)/shard_map/all_to_all | solution.py:29
  60.2 0.2 convert_reduce_fusion
  60.5 0.7 broadcast_in_dim.44
  61.2 10.0 %all-to-all-start.3 = ((bf16[8,2,1920]{2,1,0:T(2,128)(2,1)}), bf16[8,2,1920]{2,1,0:T(2,128)(2,1)S(1)}, u32[]{:S(2)}, u32[]{:S(2)}) async-start(bf16[8,2,1920]{2,1,0:T(2,128)(2,1)} %broadcast_in_dim.44), calls=%async_computation.3 | async-start | bytes 122880 | tf_op jit(solution)/shard_map/all_to_all | solution.py:29
  71.2 7.2 %all-to-all-done.3 = bf16[8,2,1920]{2,1,0:T(2,128)(2,1)S(1)} async-done(((bf16[8,2,1920]{2,1,0:T(2,128)(2,1)}), bf16[8,2,1920]{2,1,0:T(2,128)(2,1)S(1)}, u32[]{:S(2)}, u32[]{:S(2)}) %all-to-all-start.3) | async-done | bytes 61472 | tf_op jit(solution)/shard_map/all_to_all | solution.py:29
  78.4 0.0 copy-start.3
  78.4 0.1 reshape.156
  78.7 0.6 copy-done.3
  79.3 0.2 convolution_convert_fusion.4
  79.6 0.2 convolution_convert_fusion.5
  79.9 0.2 fusion.2
  80.2 0.1 broadcast_in_dim.46
  80.3 0.1 broadcast_in_dim.45
  80.4 0.3 pad_maximum_fusion.1
  80.6 19.9 %all_to_all.26 = bf16[64,2,1152]{2,1,0:T(2,128)(2,1)S(1)} all-to-all(bf16[64,2,1152]{2,1,0:T(2,128)(2,1)S(1)} %pad_maximum_fusion.1), channel_id=1, replica_groups=mesh['leaf'=8,'rows'=64] {'rows'}, dimensions={0} | all-to-all | bytes 589824 | tf_op jit(solution)/shard_map/all_to_all | solution.py:29
  100.5 0.1 slice.232
  100.6 0.1 reshape.160
  100.7 0.1 slice.227
  100.8 2.0 %collective-permute-start.1 = (bf16[128,768]{1,0:T(8,128)(2,1)S(1)}, bf16[128,768]{1,0:T(8,128)(2,1)S(1)}, u32[]{:S(2)}, u32[]{:S(2)}) collective-permute-start(bf16[128,768]{1,0:T(8,128)(2,1)S(1)} %reshape.160), channel_id=1, source_target_pairs={{0,1},{1,0},{2,3},{3,2},{4,5},{5,4},{6,7},{7,6},{8,9},{9,8},{10,11... | collective-permute-start | bytes 589832 | tf_op jit(solution)/shard_map/ppermute | solution.py:25
  102.9 0.1 fusion.20
  103.0 1.1 %collective-permute-done.1 = bf16[128,768]{1,0:T(8,128)(2,1)S(1)} collective-permute-done((bf16[128,768]{1,0:T(8,128)(2,1)S(1)}, bf16[128,768]{1,0:T(8,128)(2,1)S(1)}, u32[]{:S(2)}, u32[]{:S(2)}) %collective-permute-start.1) | collective-permute-done | bytes 196640 | tf_op jit(solution)/shard_map/ppermute | solution.py:25
  104.2 0.2 convolution_add_fusion
  104.3 0.1 fusion.28
  104.5 0.1 fusion.31
  104.6 0.9 convolution_subtract_fusion
  (53 shorter events, 0.7 us)
Async XLA Ops:
  0.0 79.6 %copy-start = (bf16[4,256,512]{2,1,0:T(8,128)(2,1)S(1)}, bf16[4,256,512]{2,1,0:T(8,128)(2,1)}, u32[]{:S(2)}) copy-start(bf16[4,256,512]{2,1,0:T(8,128)(2,1)} %param.16) | copy-start | bytes 3145732
  0.0 0.8 copy-start.5
  1.7 12.4 %copy-start.2 = (bf16[3,256,384]{2,1,0:T(8,128)(2,1)S(1)}, bf16[3,256,384]{2,1,0:T(8,128)(2,1)}, u32[]{:S(2)}) copy-start(bf16[3,256,384]{2,1,0:T(8,128)(2,1)} %param.13) | copy-start | bytes 1769476
  2.5 21.7 %all-to-all-start = ((bf16[64,4,128]{2,1,0:T(4,128)(2,1)}), bf16[64,4,128]{2,1,0:T(4,128)(2,1)S(1)}, u32[]{:S(2)}, u32[]{:S(2)}) async-start(bf16[64,4,128]{2,1,0:T(4,128)(2,1)} %pad_maximum_fusion.3), calls=%async_computation | async-start | bytes 131072 | tf_op jit(solution)/shard_map/all_to_all | solution.py:29
  14.1 1.2 %slice-start = ((bf16[3,256,384]{2,1,0:T(8,128)(2,1)}), bf16[2,256,384]{2,1,0:T(8,128)(2,1)S(1)}, s32[]{:S(2)}) async-start(bf16[3,256,384]{2,1,0:T(8,128)(2,1)} %param.14), calls=%async_computation.5 | async-start | bytes 786432 | tf_op jit(solution)/shard_map/slice | solution.py:63
  14.1 1.5 %copy-start.1 = (bf16[3,256,384]{2,1,0:T(8,128)(2,1)S(1)}, bf16[3,256,384]{2,1,0:T(8,128)(2,1)}, u32[]{:S(2)}) copy-start(bf16[3,256,384]{2,1,0:T(8,128)(2,1)} %param.14) | copy-start | bytes 1769476
  15.9 13.9 %collective-permute-start = (bf16[128,768]{1,0:T(8,128)(2,1)S(1)}, bf16[128,768]{1,0:T(8,128)(2,1)S(1)}, u32[]{:S(2)}, u32[]{:S(2)}) collective-permute-start(bf16[128,768]{1,0:T(8,128)(2,1)S(1)} %broadcast_select_fusion), channel_id=1, source_target_pairs={{0,1},{1,0},{2,3},{3,2},{4,5},{5,4},{6,7},{7,6},{8,9},{9,8},{10,11... | collective-permute-start | bytes 589832 | tf_op jit(solution)/shard_map/ppermute | solution.py:25
  25.4 15.2 %all-to-all-start.1 = ((bf16[64,2,384]{2,1,0:T(2,128)(2,1)}), bf16[64,2,384]{2,1,0:T(2,128)(2,1)S(1)}, u32[]{:S(2)}, u32[]{:S(2)}) async-start(bf16[64,2,384]{2,1,0:T(2,128)(2,1)} %reshape.149), calls=%async_computation.1 | async-start | bytes 196608 | tf_op jit(solution)/shard_map/all_to_all | solution.py:29
  61.2 17.2 %all-to-all-start.3 = ((bf16[8,2,1920]{2,1,0:T(2,128)(2,1)}), bf16[8,2,1920]{2,1,0:T(2,128)(2,1)S(1)}, u32[]{:S(2)}, u32[]{:S(2)}) async-start(bf16[8,2,1920]{2,1,0:T(2,128)(2,1)} %broadcast_in_dim.44), calls=%async_computation.3 | async-start | bytes 122880 | tf_op jit(solution)/shard_map/all_to_all | solution.py:29
  78.4 1.0 copy-start.3
  78.5 1.4 %copy-start.4 = (bf16[2,256,512]{2,1,0:T(8,128)(2,1)S(1)}, bf16[2,256,512]{2,1,0:T(8,128)(2,1)}, u32[]{:S(2)}) copy-start(bf16[2,256,512]{2,1,0:T(8,128)(2,1)} %param.15) | copy-start | bytes 1572868
  100.8 3.3 %collective-permute-start.1 = (bf16[128,768]{1,0:T(8,128)(2,1)S(1)}, bf16[128,768]{1,0:T(8,128)(2,1)S(1)}, u32[]{:S(2)}, u32[]{:S(2)}) collective-permute-start(bf16[128,768]{1,0:T(8,128)(2,1)S(1)} %reshape.160), channel_id=1, source_target_pairs={{0,1},{1,0},{2,3},{3,2},{4,5},{5,4},{6,7},{7,6},{8,9},{9,8},{10,11... | collective-permute-start | bytes 589832 | tf_op jit(solution)/shard_map/ppermute | solution.py:25

commit v4 on v3

v4 whole, which is shorter than its diff:
```python
import jax
import jax.numpy as jnp
from jax import lax
from jax.sharding import Mesh
from jax.sharding import PartitionSpec as P

NNZ = 3
LEVELS = 3
LANES = 128
CORES = 2
ROWS = ("chip", "core")
ALL = ("leaf",) + ROWS


def tip_factor(tip_tags):
    return jnp.where(tip_tags == 1, 0.6, jnp.where(tip_tags == 2, 1.8, 1.0)).astype(jnp.float32)


def dot(a, b):
    return jnp.dot(a, b, preferred_element_type=jnp.float32)


def dot_nt(a, b):
    return lax.dot_general(a, b, (((1,), (1,)), ((), ())), preferred_element_type=jnp.float32)


def swap_cores(value):
    return lax.ppermute(value, "core", [(i, i ^ 1) for i in range(CORES)])


def exchange(value, axis):
    return lax.all_to_all(value, axis, 0, 0, tiled=True)


def shards(
    right_side, tip_tags, leaf_blocks, leaf_cols, u_panels, v_panels, cap_top, cap_mid, cap_low
):
    nrhs, width = right_side.shape
    rank = u_panels.shape[1]
    half = rank // CORES
    wide = LEVELS * rank
    chips = lax.axis_size("chip")
    rows = chips * CORES
    leaves = lax.axis_size("leaf")
    leaf_pos = lax.axis_index("leaf")
    second_core = lax.axis_index("core") == 1
    late_half = leaf_pos // (leaves // 2) == 1
    late_pair = leaf_pos // 2 % 2 == 1
    bf16 = jnp.bfloat16

    def mine_theirs(lower, upper):
        return jnp.where(second_core, upper, lower), jnp.where(second_core, lower, upper)

    scaled = (right_side * tip_factor(tip_tags)[None, :]).astype(bf16)

    columns = jnp.pad(leaf_cols.astype(bf16), ((0, 0), (0, LANES - 2)))
    own_rows = jnp.concatenate(
        [
            scaled.reshape(rows, width // LANES, LANES),
            jnp.broadcast_to(columns[None], (rows, 1, LANES)),
        ],
        axis=1,
    )
    first = exchange(own_rows, ROWS)
    table = first[:, : width // LANES].reshape(rows, width)
    wanted = first[:, width // LANES, :2].astype(jnp.int32)

    u_here, v_here, _ = lax.optimization_barrier((u_panels, v_panels, own_rows))
    w_first = dot_nt(u_here[0], v_here[1:].reshape(2 * rank, width))
    w_second = dot_nt(u_here[1], v_here[2])
    w_all = jnp.concatenate([w_first, w_second], axis=1).astype(bf16)
    w_mine, w_theirs = mine_theirs(w_all[:, : wide // 2], w_all[:, wide // 2 :])

    hot = (wanted[:, :, None] == jnp.arange(rows, dtype=jnp.int32)).astype(bf16)
    picked = dot(hot.reshape(rows * 2, rows), table).astype(bf16)
    top = lax.dynamic_index_in_dim(cap_top, leaf_pos // 4, 0, keepdims=False)
    mid = lax.dynamic_index_in_dim(cap_mid, leaf_pos // 2, 0, keepdims=False)
    top, mid, w_mine, w_theirs = lax.optimization_barrier((top, mid, w_mine, w_theirs))
    w_chip = (w_mine.astype(jnp.float32) + swap_cores(w_theirs).astype(jnp.float32)).astype(bf16)
    picked, late_half, late_pair, second_core = lax.optimization_barrier(
        (picked, late_half, late_pair, second_core)
    )
    second = exchange(picked.reshape(rows, 2, width), ROWS)

    blocks = jnp.concatenate([scaled, second[:, 0], second[:, 1]], axis=1)
    field = dot(blocks, leaf_blocks.reshape(NNZ * width, width))
    partial = dot_nt(field.astype(bf16), v_panels.reshape(wide, width)).astype(bf16)

    w_chip = w_chip.reshape(CORES, chips, rank // rows, wide // 2).swapaxes(0, 1)
    third = exchange(
        jnp.concatenate(
            [partial.reshape(rows, 2, wide // 2), w_chip.reshape(rows, 2, wide)], axis=2
        ),
        ROWS,
    )
    third = third.reshape(chips, CORES, 2, 3 * wide // 2).astype(jnp.float32).sum(axis=0)
    own = third[:, :, : wide // 2].sum(axis=0)
    w_rows = third[:, :, wide // 2 :].reshape(CORES, 2 * wide)

    fourth = exchange(
        jnp.broadcast_to(
            jnp.concatenate([own, w_rows], axis=1).astype(bf16)[None], (leaves, 2, 5 * wide // 2)
        ),
        "leaf",
    ).astype(jnp.float32)
    every = fourth[:, :, : wide // 2].reshape(leaves, LEVELS, rank)
    w_every = fourth[:, :, wide // 2 :].reshape(leaves, CORES, rank // rows, wide // 2)
    w_every = w_every.swapaxes(1, 2).reshape(leaves, rank // rows, wide)

    def part(value, late):
        count = value.shape[0] // 2
        return jnp.where(late, value[count:], value[:count])

    def coupled(both, cap):
        return dot_nt(jnp.concatenate([both[1], both[0]], axis=1).astype(bf16), cap)

    halves = every[:, 0].reshape(2, leaves // 2, 1, rank).sum(axis=1)
    mid_in = jnp.concatenate([every[:, 1:2], w_every[:, :, :rank]], axis=1)
    mid_in = part(mid_in, late_half)
    mid_in = mid_in.reshape(2, 2, mid_in.shape[1], rank).sum(axis=1)
    low_in = jnp.concatenate(
        [every[:, 2:3], w_every[:, :, rank : 2 * rank], w_every[:, :, 2 * rank :]], axis=1
    )
    low_in = part(part(low_in, late_half), late_pair)
    top_out = coupled(halves, top)
    mid_out = coupled(mid_in, mid)
    low_out = coupled(low_in, cap_low[0])
    start = jnp.concatenate([top_out, mid_out[:1], low_out[:1]], axis=1).astype(bf16)
    x_rows = jnp.concatenate([mid_out[1:], low_out[1:5], low_out[5:]], axis=1).astype(bf16)

    message = jnp.concatenate([start.reshape(2, wide // 2), x_rows.reshape(2, 2 * wide)], axis=1)
    fifth_mine = exchange(jnp.broadcast_to(message[None], (chips,) + message.shape), "chip")
    fifth_theirs = swap_cores(fifth_mine)
    x_mine = fifth_mine[:, :, wide // 2 :].reshape(half, wide)
    x_theirs = fifth_theirs[:, :, wide // 2 :].reshape(half, wide)
    start = jnp.stack(
        mine_theirs(fifth_mine[:, :, : wide // 2], fifth_theirs[:, :, : wide // 2]), axis=1
    ).reshape(nrhs, wide)
    mixed_top = start[:, :rank]

    def through(mixed, at):
        mine, theirs = mine_theirs(mixed[:, :half], mixed[:, half:])
        return dot(mine, x_mine[:, at]) + dot(theirs, x_theirs[:, at])

    from_top = through(mixed_top, slice(0, 2 * rank))
    mixed_mid = (start[:, rank : 2 * rank].astype(jnp.float32) - from_top[:, :rank]).astype(bf16)
    from_mid = through(mixed_mid, slice(2 * rank, wide))
    mixed_low = (start[:, 2 * rank :].astype(jnp.float32) - from_top[:, rank:] - from_mid).astype(bf16)
    mixed = jnp.concatenate([mixed_top, mixed_mid, mixed_low], axis=1)
    return field - dot(mixed, u_panels.reshape(wide, width))


def solution(mesh):
    placed = (
        P(None, ALL),
        P(ALL),
        P(None, None, ALL),
        P(ALL, None),
        P(None, None, ALL),
        P(None, None, ALL),
        P(),
        P(),
        P("leaf", None, None),
    )
    leaves, rows = mesh.devices.shape
    split = Mesh(mesh.devices.reshape(leaves, rows // CORES, CORES), ALL)
    return jax.shard_map(
        shards, mesh=split, in_specs=placed, out_specs=P(None, ALL), check_vma=False
    )
```

time: 106 us -> 102 us (0.962)
  blocking collectives: 37.3 us -> 48.4 us
  waiting for transfers between devices: 24.7 us -> 16.2 us
  starting transfers between devices: 30.5 us -> 24.4 us
  matrix products: 4.46 us -> 3.29 us
    all_to_all x2 -> x3, blocking collectives: 37.3 us -> 48.4 us  [exchange(): return lax.all_to_all(value, axis, 0, 0, tiled=True)]
    all_to_all x3 -> x2, starting transfers between devices: 26.1 us -> 16.5 us  [exchange(): return lax.all_to_all(value, axis, 0, 0, tiled=True)]
    all_to_all x3 -> x2, waiting for transfers between devices: 23.6 us -> 15.4 us  [exchange(): return lax.all_to_all(value, axis, 0, 0, tiled=True)]
    ppermute x2, starting transfers between devices: 4.4 us -> 7.9 us  [swap_cores(): return lax.ppermute(value, 'core', [(i, i ^ 1) for i in range(CORES)])]
    dot_general x7, matrix products: 3.1 us -> 1.94 us  [dot(): return jnp.dot(a, b, preferred_element_type=jnp.float32)]
    squeeze x0 -> x1, local copies, waits for them, and re-layouts: none -> 1.07 us  [shards(): mid = lax.dynamic_index_in_dim(cap_mid, leaf_pos // 2, 0, keepdims=False)]
  transfers between devices with their start and end apart: 5 -> 4, of which waited for: 4 -> 3; matrix products, arithmetic and copies ran while one was open for 2% -> 3% of each run, Pallas kernels for 0% -> 0%
where the time goes in v4:
time: 102 us; the launch traced here: 101 us
  blocking collectives  48.4 us (47%)
  starting transfers between devices  24.4 us (24%)
  waiting for transfers between devices  16.2 us (16%)
  local copies, waits for them, and re-layouts  4.89 us (5%)
  other arithmetic  3.54 us (3%)
  matrix products  3.29 us (3%)
    all_to_all x3, blocking collectives, exchange(): return lax.all_to_all(value, axis, 0, 0, tiled=True)  48.4 us
    all_to_all x2, starting transfers between devices, exchange(): return lax.all_to_all(value, axis, 0, 0, tiled=True)  16.5 us
    all_to_all x2, waiting for transfers between devices, exchange(): return lax.all_to_all(value, axis, 0, 0, tiled=True)  15.4 us
    ppermute x2, starting transfers between devices, swap_cores(): return lax.ppermute(value, 'core', [(i, i ^ 1) for i in range(CORES)])  7.9 us
  transfers between devices with their start and end apart: 4, of which 3 were waited for; matrix products, arithmetic and copies ran while one was open for 3% of the time, Pallas kernels for 0%

profile of v4, /device:TPU:1, one launch (start us, length us, event | category | flops | bytes accessed | tf_op | source)
XLA Modules:
  0.0 101.3 jit_solution(11136708474464157310)
XLA Ops:
  0.0 0.8 convert_element_type.83
  0.8 0.9 multiply_convert_fusion
  1.8 0.7 pad_maximum_fusion.4
  2.5 11.6 %all-to-all-start = ((bf16[64,4,128]{2,1,0:T(4,128)(2,1)}), bf16[64,4,128]{2,1,0:T(4,128)(2,1)S(1)}, u32[]{:S(2)}, u32[]{:S(2)}) async-start(bf16[64,4,128]{2,1,0:T(4,128)(2,1)} %pad_maximum_fusion.4), calls=%async_computation | async-start | bytes 131072 | tf_op jit(solution)/shard_map/all_to_all | solution.py:32
  14.1 0.3 convolution_convert_fusion.1
  14.4 0.7 slice-done
  15.1 0.3 convolution_convert_fusion
  15.5 0.1 broadcast_select_fusion
  15.6 1.1 %dynamic-slice_bitcast_fusion = (bf16[256,512]{1,0:T(8,128)(2,1)S(1)}, bf16[256,512]{1,0:T(8,128)(2,1)S(1)}) fusion(bf16[4,256,512]{2,1,0:T(8,128)(2,1)} %param.16, s32[]{:T(128)S(6)} %select_n.107, bf16[2,256,512]{2,1,0:T(8,128)(2,1)} %param.15, s32[]{:T(128)S(6)} %select_n.106), kind=kLoop, calls=%fused_computation.15 | loop fusion | bytes 1048584 | tf_op jit(solution)/shard_map/jit(dynamic_index_in_dim)/squeeze | solution.py:77
  16.6 2.4 %collective-permute-start = (bf16[256,384]{1,0:T(8,128)(2,1)S(1)}, bf16[256,384]{1,0:T(8,128)(2,1)S(1)}, u32[]{:S(2)}, u32[]{:S(2)}) collective-permute-start(bf16[256,384]{1,0:T(8,128)(2,1)S(1)} %get-tuple-element.20), channel_id=1, source_target_pairs={{0,1},{1,0},{2,3},{3,2},{4,5},{5,4},{6,7},{7,6},{8,9},{9,8},{10,11... | collective-permute-start | bytes 589832 | tf_op jit(solution)/shard_map/ppermute | solution.py:28
  19.0 5.1 %all-to-all-done = bf16[64,4,128]{2,1,0:T(4,128)(2,1)S(1)} async-done(((bf16[64,4,128]{2,1,0:T(4,128)(2,1)}), bf16[64,4,128]{2,1,0:T(4,128)(2,1)S(1)}, u32[]{:S(2)}, u32[]{:S(2)}) %all-to-all-start) | async-done | bytes 65568 | tf_op jit(solution)/shard_map/all_to_all | solution.py:32
  24.2 0.1 fusion.35
  24.3 0.1 reshape.144
  24.4 0.2 convolution_convert_fusion.3
  24.7 0.7 reshape.129
  25.4 4.9 %all-to-all-start.1 = ((bf16[64,2,384]{2,1,0:T(2,128)(2,1)}), bf16[64,2,384]{2,1,0:T(2,128)(2,1)S(1)}, u32[]{:S(2)}, u32[]{:S(2)}) async-start(bf16[64,2,384]{2,1,0:T(2,128)(2,1)} %reshape.129), calls=%async_computation.1 | async-start | bytes 196608 | tf_op jit(solution)/shard_map/all_to_all | solution.py:32
  30.3 0.1 add_convert_fusion
  30.3 0.1 reshape.134
  30.4 0.1 copy.67
  30.4 0.1 reshape.135
  30.6 10.2 %all-to-all-done.1 = bf16[64,2,384]{2,1,0:T(2,128)(2,1)S(1)} async-done(((bf16[64,2,384]{2,1,0:T(2,128)(2,1)}), bf16[64,2,384]{2,1,0:T(2,128)(2,1)S(1)}, u32[]{:S(2)}, u32[]{:S(2)}) %all-to-all-start.1) | async-done | bytes 98336 | tf_op jit(solution)/shard_map/all_to_all | solution.py:32
  40.8 0.1 fusion.65
  41.0 0.3 fusion.9
  41.3 0.3 convolution_convert_fusion.2
  41.6 0.3 pad_maximum_fusion
  41.9 17.5 %all_to_all.25 = bf16[64,2,1152]{2,1,0:T(2,128)(2,1)S(1)} all-to-all(bf16[64,2,1152]{2,1,0:T(2,128)(2,1)S(1)} %pad_maximum_fusion), channel_id=1, replica_groups=mesh['leaf'=8,'chip'=32,'core'=2] {'chip','core'}, dimensions={0} | all-to-all | bytes 589824 | tf_op jit(solution)/shard_map/all_to_all | solution.py:32
  59.3 0.2 convert_reduce_fusion
  59.7 17.0 %all_to_all.26 = bf16[8,2,1920]{2,1,0:T(2,128)(2,1)S(1)} all-to-all(bf16[8,2,1920]{2,1,0:T(2,128)(2,1)S(1)} %broadcast_in_dim.40), channel_id=1, replica_groups=mesh['leaf'=8,'chip'=32,'core'=2] {'leaf'}, dimensions={0} | all-to-all | bytes 122880 | tf_op jit(solution)/shard_map/all_to_all | solution.py:32
  76.8 0.1 reshape.138
  77.0 0.1 convolution_convert_fusion.5
  77.3 0.7 copy-done.3
  78.0 0.2 convolution_convert_fusion.4
  78.2 0.1 fusion.67
  78.5 0.1 broadcast_in_dim.41
  78.7 13.9 %all_to_all.27 = bf16[32,2,1920]{2,1,0:T(2,128)(2,1)S(1)} all-to-all(bf16[32,2,1920]{2,1,0:T(2,128)(2,1)S(1)} %broadcast_in_dim.41), channel_id=1, replica_groups=mesh['leaf'=8,'chip'=32,'core'=2] {'chip'}, dimensions={0} | all-to-all | bytes 491520 | tf_op jit(solution)/shard_map/all_to_all | solution.py:32
  92.6 5.5 %collective-permute-start.1 = (bf16[32,2,1920]{2,1,0:T(2,128)(2,1)S(1)}, bf16[32,2,1920]{2,1,0:T(2,128)(2,1)S(1)}, u32[]{:S(2)}, u32[]{:S(2)}) collective-permute-start(bf16[32,2,1920]{2,1,0:T(2,128)(2,1)S(1)} %all_to_all.27), channel_id=1, source_target_pairs={{0,1},{1,0},{2,3},{3,2},{4,5},{5,4},{6,7},{7,6},{8,9},{9,8},{10,11... | collective-permute-start | bytes 737288 | tf_op jit(solution)/shard_map/ppermute | solution.py:28
  98.2 0.1 slice.271
  98.3 0.1 reshape.141
  98.4 0.8 collective-permute-done.1
  99.3 0.1 slice.273
  99.4 0.1 reshape.142
  99.5 0.1 fusion.27
  99.6 0.1 pad_maximum_fusion.3
  99.8 0.1 fusion.16
  100.0 0.2 convolution_add_fusion
  100.1 0.1 fusion.24
  100.3 0.1 fusion.1
  100.4 0.9 convolution_subtract_fusion
  (54 shorter events, 0.7 us)
Async XLA Ops:
  0.0 41.0 %copy-start = (bf16[3,384,384]{2,1,0:T(8,128)(2,1)S(1)}, bf16[3,384,384]{2,1,0:T(8,128)(2,1)}, u32[]{:S(2)}) copy-start(bf16[3,384,384]{2,1,0:T(8,128)(2,1)} %param.11) | copy-start | bytes 2654212
  0.0 0.8 copy-start.4
  1.7 12.4 %copy-start.1 = (bf16[3,256,384]{2,1,0:T(8,128)(2,1)S(1)}, bf16[3,256,384]{2,1,0:T(8,128)(2,1)}, u32[]{:S(2)}) copy-start(bf16[3,256,384]{2,1,0:T(8,128)(2,1)} %param.14) | copy-start | bytes 1769476
  1.7 12.4 %copy-start.2 = (bf16[3,256,384]{2,1,0:T(8,128)(2,1)S(1)}, bf16[3,256,384]{2,1,0:T(8,128)(2,1)}, u32[]{:S(2)}) copy-start(bf16[3,256,384]{2,1,0:T(8,128)(2,1)} %param.13) | copy-start | bytes 1769476
  2.5 21.7 %all-to-all-start = ((bf16[64,4,128]{2,1,0:T(4,128)(2,1)}), bf16[64,4,128]{2,1,0:T(4,128)(2,1)S(1)}, u32[]{:S(2)}, u32[]{:S(2)}) async-start(bf16[64,4,128]{2,1,0:T(4,128)(2,1)} %pad_maximum_fusion.4), calls=%async_computation | async-start | bytes 131072 | tf_op jit(solution)/shard_map/all_to_all | solution.py:32
  14.1 1.0 slice-start
  16.6 13.6 %collective-permute-start = (bf16[256,384]{1,0:T(8,128)(2,1)S(1)}, bf16[256,384]{1,0:T(8,128)(2,1)S(1)}, u32[]{:S(2)}, u32[]{:S(2)}) collective-permute-start(bf16[256,384]{1,0:T(8,128)(2,1)S(1)} %get-tuple-element.20), channel_id=1, source_target_pairs={{0,1},{1,0},{2,3},{3,2},{4,5},{5,4},{6,7},{7,6},{8,9},{9,8},{10,11... | collective-permute-start | bytes 589832 | tf_op jit(solution)/shard_map/ppermute | solution.py:28
  25.4 15.4 %all-to-all-start.1 = ((bf16[64,2,384]{2,1,0:T(2,128)(2,1)}), bf16[64,2,384]{2,1,0:T(2,128)(2,1)S(1)}, u32[]{:S(2)}, u32[]{:S(2)}) async-start(bf16[64,2,384]{2,1,0:T(2,128)(2,1)} %reshape.129), calls=%async_computation.1 | async-start | bytes 196608 | tf_op jit(solution)/shard_map/all_to_all | solution.py:32
  77.0 1.0 copy-start.3
  92.6 6.7 %collective-permute-start.1 = (bf16[32,2,1920]{2,1,0:T(2,128)(2,1)S(1)}, bf16[32,2,1920]{2,1,0:T(2,128)(2,1)S(1)}, u32[]{:S(2)}, u32[]{:S(2)}) collective-permute-start(bf16[32,2,1920]{2,1,0:T(2,128)(2,1)S(1)} %all_to_all.27), channel_id=1, source_target_pairs={{0,1},{1,0},{2,3},{3,2},{4,5},{5,4},{6,7},{7,6},{8,9},{9,8},{10,11... | collective-permute-start | bytes 737288 | tf_op jit(solution)/shard_map/ppermute | solution.py:28

commit v5 on v4

--- a/solution.py
+++ b/solution.py
@@ -1,6 +1,8 @@
 import jax
 import jax.numpy as jnp
 from jax import lax
+from jax.experimental import pallas as pl
+from jax.experimental.pallas import tpu as pltpu
 from jax.sharding import Mesh
 from jax.sharding import PartitionSpec as P
 
@@ -30,6 +32,73 @@
 
 def exchange(value, axis):
     return lax.all_to_all(value, axis, 0, 0, tiled=True)
+
+
+def call(kernel, inputs, scalars, *outputs):
+    vmem = pl.BlockSpec(memory_space=pltpu.VMEM)
+    smem = pl.BlockSpec(memory_space=pltpu.SMEM)
+    return pl.pallas_call(
+        kernel,
+        out_shape=[jax.ShapeDtypeStruct(*output) for output in outputs],
+        in_specs=[smem] * len(scalars) + [vmem] * len(inputs),
+        out_specs=[vmem] * len(outputs),
+        compiler_params=pltpu.CompilerParams(vmem_limit_bytes=12 * 2**20),
+    )(*scalars, *inputs)
+
+
+def solve_kernel(leaf_ref, fourth_ref, top_ref, mid_ref, low_ref, message_ref):
+    leaf_pos = leaf_ref[0, 0]
+    leaves = fourth_ref.shape[0]
+    rank = top_ref.shape[0]
+    edge = LEVELS * rank // 2
+    first = fourth_ref[:, 0, :].astype(jnp.float32)
+    second = fourth_ref[:, 1, :].astype(jnp.float32)
+    every = [
+        jnp.concatenate([first[:, at : at + edge], second[:, at : at + edge]], axis=1)
+        for at in range(0, first.shape[1], edge)
+    ]
+    subtree = lax.broadcasted_iota(jnp.int32, (leaves, rank), 0)
+
+    def stacked(value, span):
+        parent = leaf_pos // (2 * span) * 2
+
+        def child(which):
+            inside = subtree // span == parent + which
+            return jnp.sum(jnp.where(inside, value, 0.0), axis=0, keepdims=True)
+
+        return jnp.concatenate([child(1), child(0)], axis=1)
+
+    def coupled(values, span, cap):
+        rows = [stacked(value, span) for value in values]
+        rows += [jnp.zeros_like(rows[0])] * (-len(rows) % 8)
+        return dot_nt(jnp.concatenate(rows, axis=0).astype(jnp.bfloat16), cap)
+
+    def level(value, at):
+        return value[:, at * rank : (at + 1) * rank]
+
+    top_out = coupled([level(every[0], 0)], leaves // 2, top_ref[...])
+    mid_out = coupled(
+        [level(every[0], 1)] + [level(value, 0) for value in every[1:]], leaves // 4, mid_ref[...]
+    )
+    low_out = coupled(
+        [level(every[0], 2)] + [level(value, at) for at in (1, 2) for value in every[1:]],
+        leaves // 8,
+        low_ref[0],
+    )
+    count = len(every) - 1
+    start = jnp.concatenate([top_out[:1], mid_out[:1], low_out[:1]], axis=1)
+    x_rows = [
+        jnp.concatenate(
+            [mid_out[at : at + 1], low_out[at : at + 1], low_out[at + count : at + count + 1]], axis=1
+        )
+        for at in range(1, count + 1)
+    ]
+    for at in range(2):
+        row = jnp.concatenate(
+            [start[:, at * edge : (at + 1) * edge]] + x_rows[at * count // 2 : (at + 1) * count // 2],
+            axis=1,
+        ).astype(jnp.bfloat16)
+        message_ref[:, at, :] = jnp.broadcast_to(row, (message_ref.shape[0], row.shape[1]))
 
 
 def shards(
@@ -44,8 +113,6 @@
     leaves = lax.axis_size("leaf")
     leaf_pos = lax.axis_index("leaf")
     second_core = lax.axis_index("core") == 1
-    late_half = leaf_pos // (leaves // 2) == 1
-    late_pair = leaf_pos // 2 % 2 == 1
     bf16 = jnp.bfloat16
 
     def mine_theirs(lower, upper):
@@ -77,9 +144,7 @@
     mid = lax.dynamic_index_in_dim(cap_mid, leaf_pos // 2, 0, keepdims=False)
     top, mid, w_mine, w_theirs = lax.optimization_barrier((top, mid, w_mine, w_theirs))
     w_chip = (w_mine.astype(jnp.float32) + swap_cores(w_theirs).astype(jnp.float32)).astype(bf16)
-    picked, late_half, late_pair, second_core = lax.optimization_barrier(
-        (picked, late_half, late_pair, second_core)
-    )
+    picked, second_core = lax.optimization_barrier((picked, second_core))
     second = exchange(picked.reshape(rows, 2, width), ROWS)
 
     blocks = jnp.concatenate([scaled, second[:, 0], second[:, 1]], axis=1)
@@ -102,34 +167,15 @@
             jnp.concatenate([own, w_rows], axis=1).astype(bf16)[None], (leaves, 2, 5 * wide // 2)
         ),
         "leaf",
-    ).astype(jnp.float32)
-    every = fourth[:, :, : wide // 2].reshape(leaves, LEVELS, rank)
-    w_every = fourth[:, :, wide // 2 :].reshape(leaves, CORES, rank // rows, wide // 2)
-    w_every = w_every.swapaxes(1, 2).reshape(leaves, rank // rows, wide)
-
-    def part(value, late):
-        count = value.shape[0] // 2
-        return jnp.where(late, value[count:], value[:count])
-
-    def coupled(both, cap):
-        return dot_nt(jnp.concatenate([both[1], both[0]], axis=1).astype(bf16), cap)
-
-    halves = every[:, 0].reshape(2, leaves // 2, 1, rank).sum(axis=1)
-    mid_in = jnp.concatenate([every[:, 1:2], w_every[:, :, :rank]], axis=1)
-    mid_in = part(mid_in, late_half)
-    mid_in = mid_in.reshape(2, 2, mid_in.shape[1], rank).sum(axis=1)
-    low_in = jnp.concatenate(
-        [every[:, 2:3], w_every[:, :, rank : 2 * rank], w_every[:, :, 2 * rank :]], axis=1
-    )
-    low_in = part(part(low_in, late_half), late_pair)
-    top_out = coupled(halves, top)
-    mid_out = coupled(mid_in, mid)
-    low_out = coupled(low_in, cap_low[0])
-    start = jnp.concatenate([top_out, mid_out[:1], low_out[:1]], axis=1).astype(bf16)
-    x_rows = jnp.concatenate([mid_out[1:], low_out[1:5], low_out[5:]], axis=1).astype(bf16)
-
-    message = jnp.concatenate([start.reshape(2, wide // 2), x_rows.reshape(2, 2 * wide)], axis=1)
-    fifth_mine = exchange(jnp.broadcast_to(message[None], (chips,) + message.shape), "chip")
+    )
+
+    (message,) = call(
+        solve_kernel,
+        (fourth, top, mid, cap_low),
+        (leaf_pos.astype(jnp.int32).reshape(1, 1),),
+        ((chips, 2, 5 * wide // 2), bf16),
+    )
+    fifth_mine = exchange(message, "chip")
     fifth_theirs = swap_cores(fifth_mine)
     x_mine = fifth_mine[:, :, wide // 2 :].reshape(half, wide)
     x_theirs = fifth_theirs[:, :, wide // 2 :].reshape(half, wide)

time: 102 us -> 100 us (0.980)
  local copies, waits for them, and re-layouts: 4.89 us -> 3.79 us
  transfers between devices with their start and end apart: 4 -> 4, of which waited for: 3 -> 3; matrix products, arithmetic and copies ran while one was open for 3% -> 4% of each run, Pallas kernels for 0% -> 0%
where the time goes in v5:
time: 100 us; the launch traced here: 99.8 us
  blocking collectives  48.4 us (48%)
  starting transfers between devices  24.4 us (24%)
  waiting for transfers between devices  15.3 us (15%)
  other arithmetic  4.29 us (4%)
  local copies, waits for them, and re-layouts  3.79 us (4%)
  matrix products  2.83 us (3%)
    all_to_all x3, blocking collectives, exchange(): return lax.all_to_all(value, axis, 0, 0, tiled=True)  48.4 us
    all_to_all x2, starting transfers between devices, exchange(): return lax.all_to_all(value, axis, 0, 0, tiled=True)  16.5 us
    all_to_all x2, waiting for transfers between devices, exchange(): return lax.all_to_all(value, axis, 0, 0, tiled=True)  14.5 us
    ppermute x2, starting transfers between devices, swap_cores(): return lax.ppermute(value, 'core', [(i, i ^ 1) for i in range(CORES)])  7.91 us
  transfers between devices with their start and end apart: 4, of which 3 were waited for; matrix products, arithmetic and copies ran while one was open for 4% of the time, Pallas kernels for 0%

profile of v5, /device:TPU:1, one launch (start us, length us, event | category | flops | bytes accessed | tf_op | source)
XLA Modules:
  0.0 99.8 jit_solution(6773391006306349186)
XLA Ops:
  0.0 0.8 convert_element_type.62
  0.8 0.9 multiply_convert_fusion
  1.7 0.0 copy-start.2
  1.7 0.0 copy-start.3
  1.8 0.7 pad_maximum_fusion.3
  2.5 11.6 %all-to-all-start = ((bf16[64,4,128]{2,1,0:T(4,128)(2,1)}), bf16[64,4,128]{2,1,0:T(4,128)(2,1)S(1)}, u32[]{:S(2)}, u32[]{:S(2)}) async-start(bf16[64,4,128]{2,1,0:T(4,128)(2,1)} %pad_maximum_fusion.3), calls=%async_computation | async-start | bytes 131072 | tf_op jit(solution)/shard_map/all_to_all | solution.py:34
  14.1 0.0 slice-start
  14.1 0.3 convolution_convert_fusion.1
  14.4 0.7 slice-done
  15.1 0.3 convolution_convert_fusion
  15.5 0.1 broadcast_select_fusion
  15.6 1.1 %dynamic-slice_bitcast_fusion = (bf16[256,512]{1,0:T(8,128)(2,1)S(1)}, bf16[256,512]{1,0:T(8,128)(2,1)S(1)}) fusion(bf16[4,256,512]{2,1,0:T(8,128)(2,1)} %param.16, s32[]{:T(128)S(6)} %select_n.74, bf16[2,256,512]{2,1,0:T(8,128)(2,1)} %param.15, s32[]{:T(128)S(6)} %select_n.72), kind=kLoop, calls=%fused_computation.12 | loop fusion | bytes 1048584 | tf_op jit(solution)/shard_map/jit(dynamic_index_in_dim)/squeeze | solution.py:144
  16.6 2.4 %collective-permute-start = (bf16[256,384]{1,0:T(8,128)(2,1)S(1)}, bf16[256,384]{1,0:T(8,128)(2,1)}, u32[]{:S(2)}, u32[]{:S(2)}) collective-permute-start(bf16[256,384]{1,0:T(8,128)(2,1)S(1)} %get-tuple-element.18), channel_id=1, source_target_pairs={{0,1},{1,0},{2,3},{3,2},{4,5},{5,4},{6,7},{7,6},{8,9},{9,8},{10,11... | collective-permute-start | bytes 589832 | tf_op jit(solution)/shard_map/ppermute | solution.py:30
  19.0 5.2 %all-to-all-done = bf16[64,4,128]{2,1,0:T(4,128)(2,1)S(1)} async-done(((bf16[64,4,128]{2,1,0:T(4,128)(2,1)}), bf16[64,4,128]{2,1,0:T(4,128)(2,1)S(1)}, u32[]{:S(2)}, u32[]{:S(2)}) %all-to-all-start) | async-done | bytes 65568 | tf_op jit(solution)/shard_map/all_to_all | solution.py:34
  24.2 0.1 fusion.31
  24.3 0.1 reshape.91
  24.4 0.2 convolution_convert_fusion.3
  24.7 0.7 reshape.79
  25.4 4.8 %all-to-all-start.1 = ((bf16[64,2,384]{2,1,0:T(2,128)(2,1)}), bf16[64,2,384]{2,1,0:T(2,128)(2,1)S(1)}, u32[]{:S(2)}, u32[]{:S(2)}) async-start(bf16[64,2,384]{2,1,0:T(2,128)(2,1)} %reshape.79), calls=%async_computation.1 | async-start | bytes 196608 | tf_op jit(solution)/shard_map/all_to_all | solution.py:34
  30.2 0.0 collective-permute-done
  30.2 1.0 add_convert_fusion
  31.2 0.1 reshape.85
  31.3 0.1 copy.39
  31.3 0.1 reshape.86
  31.5 9.3 %all-to-all-done.1 = bf16[64,2,384]{2,1,0:T(2,128)(2,1)S(1)} async-done(((bf16[64,2,384]{2,1,0:T(2,128)(2,1)}), bf16[64,2,384]{2,1,0:T(2,128)(2,1)S(1)}, u32[]{:S(2)}, u32[]{:S(2)}) %all-to-all-start.1) | async-done | bytes 98336 | tf_op jit(solution)/shard_map/all_to_all | solution.py:34
  40.8 0.1 fusion.52
  41.0 0.3 fusion.8
  41.2 0.3 convolution_convert_fusion.2
  41.6 0.3 pad_maximum_fusion
  41.8 17.5 %all_to_all.25 = bf16[64,2,1152]{2,1,0:T(2,128)(2,1)S(1)} all-to-all(bf16[64,2,1152]{2,1,0:T(2,128)(2,1)S(1)} %pad_maximum_fusion), channel_id=1, replica_groups=mesh['leaf'=8,'chip'=32,'core'=2] {'chip','core'}, dimensions={0} | all-to-all | bytes 589824 | tf_op jit(solution)/shard_map/all_to_all | solution.py:34
  59.3 0.2 convert_reduce_fusion
  59.6 17.0 %all_to_all.26.fourth_ref = bf16[8,2,1920]{2,1,0:T(2,128)(2,1)S(1)} all-to-all(bf16[8,2,1920]{2,1,0:T(2,128)(2,1)S(1)} %broadcast_in_dim.34), channel_id=1, replica_groups=mesh['leaf'=8,'chip'=32,'core'=2] {'leaf'}, dimensions={0} | all-to-all | bytes 122880 | tf_op jit(solution)/shard_map/all_to_all | solution.py:34
  76.7 0.4 shard_map.91
  77.1 13.9 %all_to_all.27 = bf16[32,2,1920]{2,1,0:T(2,128)(2,1)S(1)} all-to-all(bf16[32,2,1920]{2,1,0:T(2,128)(2,1)S(1)} %shard_map.91), channel_id=1, replica_groups=mesh['leaf'=8,'chip'=32,'core'=2] {'chip'}, dimensions={0} | all-to-all | bytes 491520 | tf_op jit(solution)/shard_map/all_to_all | solution.py:34
  91.0 5.5 %collective-permute-start.1 = (bf16[32,2,1920]{2,1,0:T(2,128)(2,1)S(1)}, bf16[32,2,1920]{2,1,0:T(2,128)(2,1)S(1)}, u32[]{:S(2)}, u32[]{:S(2)}) collective-permute-start(bf16[32,2,1920]{2,1,0:T(2,128)(2,1)S(1)} %all_to_all.27), channel_id=1, source_target_pairs={{0,1},{1,0},{2,3},{3,2},{4,5},{5,4},{6,7},{7,6},{8,9},{9,8},{10,11... | collective-permute-start | bytes 737288 | tf_op jit(solution)/shard_map/ppermute | solution.py:30
  96.5 0.1 slice.133
  96.7 0.1 reshape.88
  96.8 0.8 collective-permute-done.1
  97.7 0.1 slice.135
  97.8 0.1 reshape.89
  97.9 0.1 fusion.26
  98.0 0.1 pad_maximum_fusion.2
  98.2 0.1 copy.25
  98.3 0.1 fusion.15
  98.4 0.2 convolution_add_fusion
  98.6 0.1 fusion.23
  98.7 0.1 fusion.1
  98.9 0.9 convolution_subtract_fusion
  (22 shorter events, 0.2 us)
Async XLA Ops:
  0.0 40.9 %copy-start = (bf16[3,384,384]{2,1,0:T(8,128)(2,1)S(1)}, bf16[3,384,384]{2,1,0:T(8,128)(2,1)}, u32[]{:S(2)}) copy-start(bf16[3,384,384]{2,1,0:T(8,128)(2,1)} %param.11) | copy-start | bytes 2654212
  0.0 0.8 copy-start.4
  1.7 12.4 %copy-start.2 = (bf16[3,256,384]{2,1,0:T(8,128)(2,1)S(1)}, bf16[3,256,384]{2,1,0:T(8,128)(2,1)}, u32[]{:S(2)}) copy-start(bf16[3,256,384]{2,1,0:T(8,128)(2,1)} %param.14) | copy-start | bytes 1769476
  1.7 12.4 %copy-start.3 = (bf16[3,256,384]{2,1,0:T(8,128)(2,1)S(1)}, bf16[3,256,384]{2,1,0:T(8,128)(2,1)}, u32[]{:S(2)}) copy-start(bf16[3,256,384]{2,1,0:T(8,128)(2,1)} %param.13) | copy-start | bytes 1769476
  2.5 21.7 %all-to-all-start = ((bf16[64,4,128]{2,1,0:T(4,128)(2,1)}), bf16[64,4,128]{2,1,0:T(4,128)(2,1)S(1)}, u32[]{:S(2)}, u32[]{:S(2)}) async-start(bf16[64,4,128]{2,1,0:T(4,128)(2,1)} %pad_maximum_fusion.3), calls=%async_computation | async-start | bytes 131072 | tf_op jit(solution)/shard_map/all_to_all | solution.py:34
  14.1 1.0 %slice-start = ((bf16[3,256,384]{2,1,0:T(8,128)(2,1)}), bf16[2,256,384]{2,1,0:T(8,128)(2,1)S(1)}, s32[]{:S(2)}) async-start(bf16[3,256,384]{2,1,0:T(8,128)(2,1)} %param.14), calls=%async_computation.5 | async-start | bytes 786432 | tf_op jit(solution)/shard_map/slice | solution.py:136
  16.6 13.6 %collective-permute-start = (bf16[256,384]{1,0:T(8,128)(2,1)S(1)}, bf16[256,384]{1,0:T(8,128)(2,1)}, u32[]{:S(2)}, u32[]{:S(2)}) collective-permute-start(bf16[256,384]{1,0:T(8,128)(2,1)S(1)} %get-tuple-element.18), channel_id=1, source_target_pairs={{0,1},{1,0},{2,3},{3,2},{4,5},{5,4},{6,7},{7,6},{8,9},{9,8},{10,11... | collective-permute-start | bytes 589832 | tf_op jit(solution)/shard_map/ppermute | solution.py:30
  25.4 15.4 %all-to-all-start.1 = ((bf16[64,2,384]{2,1,0:T(2,128)(2,1)}), bf16[64,2,384]{2,1,0:T(2,128)(2,1)S(1)}, u32[]{:S(2)}, u32[]{:S(2)}) async-start(bf16[64,2,384]{2,1,0:T(2,128)(2,1)} %reshape.79), calls=%async_computation.1 | async-start | bytes 196608 | tf_op jit(solution)/shard_map/all_to_all | solution.py:34
  59.3 17.4 %copy-start.1 = (bf16[1,256,512]{2,1,0:T(8,128)(2,1)S(1)}, bf16[1,256,512]{2,1,0:T(8,128)(2,1)}, u32[]{:S(2)}) copy-start(bf16[1,256,512]{2,1,0:T(8,128)(2,1)} %low_ref.1) | copy-start | bytes 786436
  91.0 6.7 %collective-permute-start.1 = (bf16[32,2,1920]{2,1,0:T(2,128)(2,1)S(1)}, bf16[32,2,1920]{2,1,0:T(2,128)(2,1)S(1)}, u32[]{:S(2)}, u32[]{:S(2)}) collective-permute-start(bf16[32,2,1920]{2,1,0:T(2,128)(2,1)S(1)} %all_to_all.27), channel_id=1, source_target_pairs={{0,1},{1,0},{2,3},{3,2},{4,5},{5,4},{6,7},{7,6},{8,9},{9,8},{10,11... | collective-permute-start | bytes 737288 | tf_op jit(solution)/shard_map/ppermute | solution.py:30

commit v6 on v5

--- a/solution.py
+++ b/solution.py
@@ -44,6 +44,18 @@
         out_specs=[vmem] * len(outputs),
         compiler_params=pltpu.CompilerParams(vmem_limit_bytes=12 * 2**20),
     )(*scalars, *inputs)
+
+
+def leaf_kernel(scaled_ref, second_ref, leaf_ref, v_ref, w_ref, field_ref, message_ref):
+    edge = v_ref.shape[0] // 2
+    field = dot(scaled_ref[...], leaf_ref[0])
+    for slot in range(NNZ - 1):
+        field += dot(second_ref[:, slot, :], leaf_ref[slot + 1])
+    field_ref[...] = field
+    partial = dot_nt(field.astype(jnp.bfloat16), v_ref[...]).astype(jnp.bfloat16)
+    for at in range(2):
+        message_ref[:, at, :edge] = partial[:, at * edge : (at + 1) * edge]
+    message_ref[:, :, edge:] = w_ref[...]
 
 
 def solve_kernel(leaf_ref, fourth_ref, top_ref, mid_ref, low_ref, message_ref):
@@ -140,24 +152,24 @@
 
     hot = (wanted[:, :, None] == jnp.arange(rows, dtype=jnp.int32)).astype(bf16)
     picked = dot(hot.reshape(rows * 2, rows), table).astype(bf16)
-    top = lax.dynamic_index_in_dim(cap_top, leaf_pos // 4, 0, keepdims=False)
-    mid = lax.dynamic_index_in_dim(cap_mid, leaf_pos // 2, 0, keepdims=False)
-    top, mid, w_mine, w_theirs = lax.optimization_barrier((top, mid, w_mine, w_theirs))
+    tops, mids, picked = lax.optimization_barrier((cap_top, cap_mid, picked))
+    top = lax.dynamic_index_in_dim(tops, leaf_pos // 4, 0, keepdims=False)
+    mid = lax.dynamic_index_in_dim(mids, leaf_pos // 2, 0, keepdims=False)
+    w_mine, w_theirs = lax.optimization_barrier((w_mine, w_theirs))
     w_chip = (w_mine.astype(jnp.float32) + swap_cores(w_theirs).astype(jnp.float32)).astype(bf16)
-    picked, second_core = lax.optimization_barrier((picked, second_core))
+    top, mid, w_chip = lax.optimization_barrier((top, mid, w_chip))
     second = exchange(picked.reshape(rows, 2, width), ROWS)
 
-    blocks = jnp.concatenate([scaled, second[:, 0], second[:, 1]], axis=1)
-    field = dot(blocks, leaf_blocks.reshape(NNZ * width, width))
-    partial = dot_nt(field.astype(bf16), v_panels.reshape(wide, width)).astype(bf16)
-
     w_chip = w_chip.reshape(CORES, chips, rank // rows, wide // 2).swapaxes(0, 1)
-    third = exchange(
-        jnp.concatenate(
-            [partial.reshape(rows, 2, wide // 2), w_chip.reshape(rows, 2, wide)], axis=2
-        ),
-        ROWS,
-    )
+    field, message = call(
+        leaf_kernel,
+        (scaled, second, leaf_blocks, v_panels.reshape(wide, width), w_chip.reshape(rows, 2, wide)),
+        (),
+        ((nrhs, width), jnp.float32),
+        ((rows, 2, 3 * wide // 2), bf16),
+    )
+
+    third = exchange(message, ROWS)
     third = third.reshape(chips, CORES, 2, 3 * wide // 2).astype(jnp.float32).sum(axis=0)
     own = third[:, :, : wide // 2].sum(axis=0)
     w_rows = third[:, :, wide // 2 :].reshape(CORES, 2 * wide)

time: 100 us -> 99.6 us (level)
  other arithmetic: 4.29 us -> 3.03 us
  waiting for transfers between devices: 15.3 us -> 16.3 us
    all_to_all x2, waiting for transfers between devices: 14.5 us -> 15.5 us  [exchange(): return lax.all_to_all(value, axis, 0, 0, tiled=True)]
  transfers between devices with their start and end apart: 4 -> 4, of which waited for: 3 -> 3; matrix products, arithmetic and copies ran while one was open for 4% -> 3% of each run, Pallas kernels for 0% -> 0%
where the time goes in v6:
time: 99.6 us; the launch traced here: 99.1 us
  blocking collectives  48.4 us (49%)
  starting transfers between devices  24.1 us (24%)
  waiting for transfers between devices  16.3 us (16%)
  local copies, waits for them, and re-layouts  3.54 us (4%)
  other arithmetic  3.03 us (3%)
  matrix products  2.25 us (2%)
  Pallas kernels  1.12 us (1%)
    all_to_all x3, blocking collectives, exchange(): return lax.all_to_all(value, axis, 0, 0, tiled=True)  48.4 us
    all_to_all x2, starting transfers between devices, exchange(): return lax.all_to_all(value, axis, 0, 0, tiled=True)  16.1 us
    all_to_all x2, waiting for transfers between devices, exchange(): return lax.all_to_all(value, axis, 0, 0, tiled=True)  15.5 us
    ppermute x2, starting transfers between devices, swap_cores(): return lax.ppermute(value, 'core', [(i, i ^ 1) for i in range(CORES)])  8.05 us
  transfers between devices with their start and end apart: 4, of which 3 were waited for; matrix products, arithmetic and copies ran while one was open for 3% of the time, Pallas kernels for 0%

profile of v6, /device:TPU:1, one launch (start us, length us, event | category | flops | bytes accessed | tf_op | source)
XLA Modules:
  0.0 99.1 jit_solution(17692292728213854242)
XLA Ops:
  0.0 0.7 convert_element_type.56
  0.7 0.0 copy-done.5
  0.7 0.9 multiply_convert_fusion.scaled_ref
  1.6 0.0 copy-start
  1.6 0.0 copy-start.3
  1.7 0.7 pad_maximum_fusion.2
  2.4 11.6 %all-to-all-start = ((bf16[64,4,128]{2,1,0:T(4,128)(2,1)}), bf16[64,4,128]{2,1,0:T(4,128)(2,1)S(1)}, u32[]{:S(2)}, u32[]{:S(2)}) async-start(bf16[64,4,128]{2,1,0:T(4,128)(2,1)} %pad_maximum_fusion.2), calls=%async_computation | async-start | bytes 131072 | tf_op jit(solution)/shard_map/all_to_all | solution.py:34
  14.0 0.0 slice-start
  14.1 0.3 convolution_convert_fusion.1
  14.3 0.7 slice-done
  15.0 0.3 convolution_convert_fusion
  15.4 0.1 broadcast_select_fusion
  15.5 0.0 copy-start.4
  15.5 2.5 %collective-permute-start = (bf16[256,384]{1,0:T(8,128)(2,1)S(1)}, bf16[256,384]{1,0:T(8,128)(2,1)S(1)}, u32[]{:S(2)}, u32[]{:S(2)}) collective-permute-start(bf16[256,384]{1,0:T(8,128)(2,1)S(1)} %get-tuple-element.23), channel_id=1, source_target_pairs={{0,1},{1,0},{2,3},{3,2},{4,5},{5,4},{6,7},{7,6},{8,9},{9,8},{10,11... | collective-permute-start | bytes 589832 | tf_op jit(solution)/shard_map/ppermute | solution.py:30
  18.0 6.1 %all-to-all-done = bf16[64,4,128]{2,1,0:T(4,128)(2,1)S(1)} async-done(((bf16[64,4,128]{2,1,0:T(4,128)(2,1)}), bf16[64,4,128]{2,1,0:T(4,128)(2,1)S(1)}, u32[]{:S(2)}, u32[]{:S(2)}) %all-to-all-start) | async-done | bytes 65568 | tf_op jit(solution)/shard_map/all_to_all | solution.py:34
  24.1 0.1 fusion.24
  24.2 0.1 reshape.83
  24.4 0.2 convolution_convert_fusion.2
  24.6 0.7 reshape.73
  25.3 4.4 %all-to-all-start.1 = ((bf16[64,2,384]{2,1,0:T(2,128)(2,1)}), bf16[64,2,384]{2,1,0:T(2,128)(2,1)S(1)}, u32[]{:S(2)}, u32[]{:S(2)}) async-start(bf16[64,2,384]{2,1,0:T(2,128)(2,1)} %reshape.73), calls=%async_computation.1 | async-start | bytes 196608 | tf_op jit(solution)/shard_map/all_to_all | solution.py:34
  29.7 1.0 %dynamic-slice_bitcast_fusion = (bf16[256,512]{1,0:T(8,128)(2,1)S(1)}, bf16[256,512]{1,0:T(8,128)(2,1)S(1)}) fusion(bf16[4,256,512]{2,1,0:T(8,128)(2,1)} %param.16, s32[]{:T(128)S(6)} %select_n.73, bf16[2,256,512]{2,1,0:T(8,128)(2,1)S(1)} %copy-done.4, s32[]{:T(128)S(6)} %select_n.71), kind=kLoop, calls=%fused_computation.10 | loop fusion | bytes 1048584 | tf_op jit(solution)/shard_map/jit(dynamic_index_in_dim)/squeeze | solution.py:157
  30.7 0.0 copy-start.1
  30.8 0.0 collective-permute-done
  30.8 0.1 add_convert_fusion
  30.8 0.1 reshape.76
  30.9 0.1 copy.25
  31.0 0.1 reshape.77.w_ref
  31.1 9.4 %all-to-all-done.1.second_ref = bf16[64,2,384]{2,1,0:T(2,128)(2,1)S(1)} async-done(((bf16[64,2,384]{2,1,0:T(2,128)(2,1)}), bf16[64,2,384]{2,1,0:T(2,128)(2,1)S(1)}, u32[]{:S(2)}, u32[]{:S(2)}) %all-to-all-start.1) | async-done | bytes 98336 | tf_op jit(solution)/shard_map/all_to_all | solution.py:34
  40.5 0.7 shard_map.91
  41.2 17.4 %all_to_all.25 = bf16[64,2,1152]{2,1,0:T(2,128)(2,1)S(1)} all-to-all(bf16[64,2,1152]{2,1,0:T(2,128)(2,1)S(1)} %get-tuple-element.26), channel_id=1, replica_groups=mesh['leaf'=8,'chip'=32,'core'=2] {'chip','core'}, dimensions={0} | all-to-all | bytes 589824 | tf_op jit(solution)/shard_map/all_to_all | solution.py:34
  58.6 0.2 convert_reduce_fusion
  59.0 17.0 %all_to_all.26.fourth_ref = bf16[8,2,1920]{2,1,0:T(2,128)(2,1)S(1)} all-to-all(bf16[8,2,1920]{2,1,0:T(2,128)(2,1)S(1)} %broadcast_in_dim.34), channel_id=1, replica_groups=mesh['leaf'=8,'chip'=32,'core'=2] {'leaf'}, dimensions={0} | all-to-all | bytes 122880 | tf_op jit(solution)/shard_map/all_to_all | solution.py:34
  76.0 0.4 shard_map.92
  76.4 14.0 %all_to_all.27 = bf16[32,2,1920]{2,1,0:T(2,128)(2,1)S(1)} all-to-all(bf16[32,2,1920]{2,1,0:T(2,128)(2,1)S(1)} %shard_map.92), channel_id=1, replica_groups=mesh['leaf'=8,'chip'=32,'core'=2] {'chip'}, dimensions={0} | all-to-all | bytes 491520 | tf_op jit(solution)/shard_map/all_to_all | solution.py:34
  90.3 5.6 %collective-permute-start.1 = (bf16[32,2,1920]{2,1,0:T(2,128)(2,1)S(1)}, bf16[32,2,1920]{2,1,0:T(2,128)(2,1)S(1)}, u32[]{:S(2)}, u32[]{:S(2)}) collective-permute-start(bf16[32,2,1920]{2,1,0:T(2,128)(2,1)S(1)} %all_to_all.27), channel_id=1, source_target_pairs={{0,1},{1,0},{2,3},{3,2},{4,5},{5,4},{6,7},{7,6},{8,9},{9,8},{10,11... | collective-permute-start | bytes 737288 | tf_op jit(solution)/shard_map/ppermute | solution.py:30
  95.9 0.1 slice.123
  96.0 0.1 reshape.80
  96.2 0.8 collective-permute-done.1
  97.0 0.1 slice.125
  97.2 0.1 reshape.81
  97.3 0.1 fusion.20
  97.4 0.1 pad_maximum_fusion.1
  97.5 0.1 copy.15
  97.6 0.1 fusion.9
  97.8 0.2 convolution_add_fusion
  98.0 0.1 fusion.17
  98.1 0.1 fusion.1
  98.2 0.9 convolution_subtract_fusion
  (19 shorter events, 0.2 us)
Async XLA Ops:
  0.0 0.7 copy-start.5
  1.6 12.4 %copy-start = (bf16[3,256,384]{2,1,0:T(8,128)(2,1)S(1)}, bf16[3,256,384]{2,1,0:T(8,128)(2,1)}, u32[]{:S(2)}) copy-start(bf16[3,256,384]{2,1,0:T(8,128)(2,1)} %param.14) | copy-start | bytes 1769476
  1.6 12.4 %copy-start.3 = (bf16[3,256,384]{2,1,0:T(8,128)(2,1)S(1)}, bf16[3,256,384]{2,1,0:T(8,128)(2,1)}, u32[]{:S(2)}) copy-start(bf16[3,256,384]{2,1,0:T(8,128)(2,1)} %param.13) | copy-start | bytes 1769476
  2.4 21.7 %all-to-all-start = ((bf16[64,4,128]{2,1,0:T(4,128)(2,1)}), bf16[64,4,128]{2,1,0:T(4,128)(2,1)S(1)}, u32[]{:S(2)}, u32[]{:S(2)}) async-start(bf16[64,4,128]{2,1,0:T(4,128)(2,1)} %pad_maximum_fusion.2), calls=%async_computation | async-start | bytes 131072 | tf_op jit(solution)/shard_map/all_to_all | solution.py:34
  14.0 1.0 %slice-start = ((bf16[3,256,384]{2,1,0:T(8,128)(2,1)}), bf16[2,256,384]{2,1,0:T(8,128)(2,1)S(1)}, s32[]{:S(2)}) async-start(bf16[3,256,384]{2,1,0:T(8,128)(2,1)} %param.14), calls=%async_computation.5 | async-start | bytes 786432 | tf_op jit(solution)/shard_map/slice | solution.py:148
  15.5 14.3 %copy-start.4 = (bf16[2,256,512]{2,1,0:T(8,128)(2,1)S(1)}, bf16[2,256,512]{2,1,0:T(8,128)(2,1)}, u32[]{:S(2)}) copy-start(bf16[2,256,512]{2,1,0:T(8,128)(2,1)} %param.15) | copy-start | bytes 1572868
  15.5 15.3 %collective-permute-start = (bf16[256,384]{1,0:T(8,128)(2,1)S(1)}, bf16[256,384]{1,0:T(8,128)(2,1)S(1)}, u32[]{:S(2)}, u32[]{:S(2)}) collective-permute-start(bf16[256,384]{1,0:T(8,128)(2,1)S(1)} %get-tuple-element.23), channel_id=1, source_target_pairs={{0,1},{1,0},{2,3},{3,2},{4,5},{5,4},{6,7},{7,6},{8,9},{9,8},{10,11... | collective-permute-start | bytes 589832 | tf_op jit(solution)/shard_map/ppermute | solution.py:30
  25.3 15.2 %all-to-all-start.1 = ((bf16[64,2,384]{2,1,0:T(2,128)(2,1)}), bf16[64,2,384]{2,1,0:T(2,128)(2,1)S(1)}, u32[]{:S(2)}, u32[]{:S(2)}) async-start(bf16[64,2,384]{2,1,0:T(2,128)(2,1)} %reshape.73), calls=%async_computation.1 | async-start | bytes 196608 | tf_op jit(solution)/shard_map/all_to_all | solution.py:34
  30.7 9.7 %copy-start.1 = (bf16[3,384,384]{2,1,0:T(8,128)(2,1)S(1)}, bf16[3,384,384]{2,1,0:T(8,128)(2,1)}, u32[]{:S(2)}) copy-start(bf16[3,384,384]{2,1,0:T(8,128)(2,1)} %leaf_ref.1) | copy-start | bytes 2654212
  58.6 17.3 %copy-start.2 = (bf16[1,256,512]{2,1,0:T(8,128)(2,1)S(1)}, bf16[1,256,512]{2,1,0:T(8,128)(2,1)}, u32[]{:S(2)}) copy-start(bf16[1,256,512]{2,1,0:T(8,128)(2,1)} %low_ref.1) | copy-start | bytes 786436
  90.3 6.7 %collective-permute-start.1 = (bf16[32,2,1920]{2,1,0:T(2,128)(2,1)S(1)}, bf16[32,2,1920]{2,1,0:T(2,128)(2,1)S(1)}, u32[]{:S(2)}, u32[]{:S(2)}) collective-permute-start(bf16[32,2,1920]{2,1,0:T(2,128)(2,1)S(1)} %all_to_all.27), channel_id=1, source_target_pairs={{0,1},{1,0},{2,3},{3,2},{4,5},{5,4},{6,7},{7,6},{8,9},{9,8},{10,11... | collective-permute-start | bytes 737288 | tf_op jit(solution)/shard_map/ppermute | solution.py:30

commit v7 on v6

--- a/solution.py
+++ b/solution.py
@@ -113,12 +113,44 @@
         message_ref[:, at, :] = jnp.broadcast_to(row, (message_ref.shape[0], row.shape[1]))
 
 
+def finish_kernel(core_ref, mine_ref, theirs_ref, field_ref, u_ref, solution_ref):
+    second_core = core_ref[0, 0] == 1
+    wide = u_ref.shape[0]
+    rank = wide // LEVELS
+    half = rank // CORES
+    edge = wide // 2
+
+    def start_of(ref):
+        return jnp.concatenate([ref[:, 0, :edge], ref[:, 1, :edge]], axis=1).astype(jnp.float32)
+
+    def x_of(ref):
+        return ref[:, :, edge:].astype(jnp.float32).reshape(half, wide).astype(jnp.bfloat16)
+
+    x_mine, x_theirs = x_of(mine_ref), x_of(theirs_ref)
+    start_mine, start_theirs = start_of(mine_ref), start_of(theirs_ref)
+    first = jnp.where(second_core, start_theirs, start_mine)
+    second = jnp.where(second_core, start_mine, start_theirs)
+    start = jnp.stack([first, second], axis=1).reshape(2 * first.shape[0], wide)
+
+    def through(mixed, at):
+        lower, upper = mixed[:, :half], mixed[:, half:]
+        mine = jnp.where(second_core, upper, lower).astype(jnp.bfloat16)
+        theirs = jnp.where(second_core, lower, upper).astype(jnp.bfloat16)
+        return dot(mine, x_mine[:, at]) + dot(theirs, x_theirs[:, at])
+
+    from_top = through(start[:, :rank], slice(0, 2 * rank))
+    mixed_mid = start[:, rank : 2 * rank] - from_top[:, :rank]
+    from_mid = through(mixed_mid, slice(2 * rank, wide))
+    mixed_low = start[:, 2 * rank :] - from_top[:, rank:] - from_mid
+    mixed = jnp.concatenate([start[:, :rank], mixed_mid, mixed_low], axis=1).astype(jnp.bfloat16)
+    solution_ref[...] = field_ref[...] - dot(mixed, u_ref[...])
+
+
 def shards(
     right_side, tip_tags, leaf_blocks, leaf_cols, u_panels, v_panels, cap_top, cap_mid, cap_low
 ):
     nrhs, width = right_side.shape
     rank = u_panels.shape[1]
-    half = rank // CORES
     wide = LEVELS * rank
     chips = lax.axis_size("chip")
     rows = chips * CORES
@@ -189,23 +221,13 @@
     )
     fifth_mine = exchange(message, "chip")
     fifth_theirs = swap_cores(fifth_mine)
-    x_mine = fifth_mine[:, :, wide // 2 :].reshape(half, wide)
-    x_theirs = fifth_theirs[:, :, wide // 2 :].reshape(half, wide)
-    start = jnp.stack(
-        mine_theirs(fifth_mine[:, :, : wide // 2], fifth_theirs[:, :, : wide // 2]), axis=1
-    ).reshape(nrhs, wide)
-    mixed_top = start[:, :rank]
-
-    def through(mixed, at):
-        mine, theirs = mine_theirs(mixed[:, :half], mixed[:, half:])
-        return dot(mine, x_mine[:, at]) + dot(theirs, x_theirs[:, at])
-
-    from_top = through(mixed_top, slice(0, 2 * rank))
-    mixed_mid = (start[:, rank : 2 * rank].astype(jnp.float32) - from_top[:, :rank]).astype(bf16)
-    from_mid = through(mixed_mid, slice(2 * rank, wide))
-    mixed_low = (start[:, 2 * rank :].astype(jnp.float32) - from_top[:, rank:] - from_mid).astype(bf16)
-    mixed = jnp.concatenate([mixed_top, mixed_mid, mixed_low], axis=1)
-    return field - dot(mixed, u_panels.reshape(wide, width))
+    (result,) = call(
+        finish_kernel,
+        (fifth_mine, fifth_theirs, field, u_panels.reshape(wide, width)),
+        (lax.axis_index("core").astype(jnp.int32).reshape(1, 1),),
+        ((nrhs, width), jnp.float32),
+    )
+    return result
 
 
 def solution(mesh):

time: 99.6 us -> 99.4 us (level)
  Pallas kernels: 1.12 us -> 2.99 us
  matrix products: 2.25 us -> 0.81 us
    pallas_call x2 -> x3, Pallas kernels: 1.12 us -> 2.99 us  [call(): pl.pallas_call(kernel, out_shape=[jax.ShapeDtypeStruct(*output) for outpu...]
    dot_general x6 -> x1, matrix products: 1.67 us -> 0.23 us  [dot(): return jnp.dot(a, b, preferred_element_type=jnp.float32)]
where the time goes in v7:
time: 99.4 us; the launch traced here: 98.9 us
  blocking collectives  48.4 us (49%)
  starting transfers between devices  24.1 us (24%)
  waiting for transfers between devices  16.6 us (17%)
  Pallas kernels  2.99 us (3%)
  local copies, waits for them, and re-layouts  2.92 us (3%)
  other arithmetic  2.81 us (3%)
    all_to_all x3, blocking collectives, exchange(): return lax.all_to_all(value, axis, 0, 0, tiled=True)  48.4 us
    all_to_all x2, starting transfers between devices, exchange(): return lax.all_to_all(value, axis, 0, 0, tiled=True)  16.1 us
    all_to_all x2, waiting for transfers between devices, exchange(): return lax.all_to_all(value, axis, 0, 0, tiled=True)  15.5 us
    ppermute x2, starting transfers between devices, swap_cores(): return lax.ppermute(value, 'core', [(i, i ^ 1) for i in range(CORES)])  8.05 us
    pallas_call x3, Pallas kernels, call(): pl.pallas_call(kernel, out_shape=[jax.ShapeDtypeStruct(*output) for outpu...  2.99 us
  transfers between devices with their start and end apart: 4, of which 3 were waited for; matrix products, arithmetic and copies ran while one was open for 3% of the time, Pallas kernels for 0%

profile of v7, /device:TPU:1, one launch (start us, length us, event | category | flops | bytes accessed | tf_op | source)
XLA Modules:
  0.0 98.9 jit_solution(11909128525704478120)
XLA Ops:
  0.0 0.0 copy-start.5
  0.0 0.7 convert_element_type.44
  0.7 0.0 copy-done.5
  0.7 0.9 multiply_convert_fusion.scaled_ref
  1.6 0.0 copy-start
  1.6 0.0 copy-start.1
  1.7 0.7 pad_maximum_fusion.1
  2.4 11.6 %all-to-all-start = ((bf16[64,4,128]{2,1,0:T(4,128)(2,1)}), bf16[64,4,128]{2,1,0:T(4,128)(2,1)S(1)}, u32[]{:S(2)}, u32[]{:S(2)}) async-start(bf16[64,4,128]{2,1,0:T(4,128)(2,1)} %pad_maximum_fusion.1), calls=%async_computation | async-start | bytes 131072 | tf_op jit(solution)/shard_map/all_to_all | solution.py:34
  14.0 0.0 copy-done
  14.0 0.0 copy-done.1
  14.0 0.0 slice-start
  14.0 0.3 convolution_convert_fusion.1
  14.3 0.7 slice-done
  15.0 0.3 convolution_convert_fusion
  15.4 0.1 broadcast_select_fusion
  15.5 0.0 copy-start.4
  15.5 2.5 %collective-permute-start = (bf16[256,384]{1,0:T(8,128)(2,1)S(1)}, bf16[256,384]{1,0:T(8,128)(2,1)S(1)}, u32[]{:S(2)}, u32[]{:S(2)}) collective-permute-start(bf16[256,384]{1,0:T(8,128)(2,1)S(1)} %get-tuple-element.23), channel_id=1, source_target_pairs={{0,1},{1,0},{2,3},{3,2},{4,5},{5,4},{6,7},{7,6},{8,9},{9,8},{10,11... | collective-permute-start | bytes 589832 | tf_op jit(solution)/shard_map/ppermute | solution.py:30
  18.0 6.1 %all-to-all-done = bf16[64,4,128]{2,1,0:T(4,128)(2,1)S(1)} async-done(((bf16[64,4,128]{2,1,0:T(4,128)(2,1)}), bf16[64,4,128]{2,1,0:T(4,128)(2,1)S(1)}, u32[]{:S(2)}, u32[]{:S(2)}) %all-to-all-start) | async-done | bytes 65568 | tf_op jit(solution)/shard_map/all_to_all | solution.py:34
  24.1 0.1 fusion.8
  24.2 0.1 reshape.75
  24.4 0.2 convolution_convert_fusion.2
  24.6 0.7 reshape.69
  25.3 4.4 %all-to-all-start.1 = ((bf16[64,2,384]{2,1,0:T(2,128)(2,1)}), bf16[64,2,384]{2,1,0:T(2,128)(2,1)S(1)}, u32[]{:S(2)}, u32[]{:S(2)}) async-start(bf16[64,2,384]{2,1,0:T(2,128)(2,1)} %reshape.69), calls=%async_computation.1 | async-start | bytes 196608 | tf_op jit(solution)/shard_map/all_to_all | solution.py:34
  29.7 0.0 copy-done.4
  29.7 1.0 %dynamic-slice_bitcast_fusion = (bf16[256,512]{1,0:T(8,128)(2,1)S(1)}, bf16[256,512]{1,0:T(8,128)(2,1)S(1)}) fusion(bf16[4,256,512]{2,1,0:T(8,128)(2,1)} %param.16, s32[]{:T(128)S(6)} %select_n.41, bf16[2,256,512]{2,1,0:T(8,128)(2,1)S(1)} %copy-done.4, s32[]{:T(128)S(6)} %select_n.39), kind=kLoop, calls=%fused_computation.5 | loop fusion | bytes 1048584 | tf_op jit(solution)/shard_map/jit(dynamic_index_in_dim)/squeeze | solution.py:189
  30.7 0.0 copy-start.2
  30.7 0.0 collective-permute-done
  30.8 0.1 add_convert_fusion
  30.8 0.1 reshape.72
  30.9 0.1 copy.23
  31.0 0.1 reshape.73.w_ref
  31.1 9.4 %all-to-all-done.1.second_ref = bf16[64,2,384]{2,1,0:T(2,128)(2,1)S(1)} async-done(((bf16[64,2,384]{2,1,0:T(2,128)(2,1)}), bf16[64,2,384]{2,1,0:T(2,128)(2,1)S(1)}, u32[]{:S(2)}, u32[]{:S(2)}) %all-to-all-start.1) | async-done | bytes 98336 | tf_op jit(solution)/shard_map/all_to_all | solution.py:34
  40.5 0.0 copy-done.2
  40.5 0.7 shard_map.91
  41.2 17.4 %all_to_all.25 = bf16[64,2,1152]{2,1,0:T(2,128)(2,1)S(1)} all-to-all(bf16[64,2,1152]{2,1,0:T(2,128)(2,1)S(1)} %get-tuple-element.25), channel_id=1, replica_groups=mesh['leaf'=8,'chip'=32,'core'=2] {'chip','core'}, dimensions={0} | all-to-all | bytes 589824 | tf_op jit(solution)/shard_map/all_to_all | solution.py:34
  58.6 0.0 copy-start.3
  58.6 0.2 convert_reduce_fusion
  59.0 17.0 %all_to_all.26.fourth_ref = bf16[8,2,1920]{2,1,0:T(2,128)(2,1)S(1)} all-to-all(bf16[8,2,1920]{2,1,0:T(2,128)(2,1)S(1)} %broadcast_in_dim.34), channel_id=1, replica_groups=mesh['leaf'=8,'chip'=32,'core'=2] {'leaf'}, dimensions={0} | all-to-all | bytes 122880 | tf_op jit(solution)/shard_map/all_to_all | solution.py:34
  76.0 0.0 copy-done.3
  76.0 0.4 shard_map.92
  76.4 14.0 %all_to_all.27.mine_ref = bf16[32,2,1920]{2,1,0:T(2,128)(2,1)S(1)} all-to-all(bf16[32,2,1920]{2,1,0:T(2,128)(2,1)S(1)} %shard_map.92), channel_id=1, replica_groups=mesh['leaf'=8,'chip'=32,'core'=2] {'chip'}, dimensions={0} | all-to-all | bytes 491520 | tf_op jit(solution)/shard_map/all_to_all | solution.py:34
  90.3 5.6 %collective-permute-start.1 = (bf16[32,2,1920]{2,1,0:T(2,128)(2,1)S(1)}, bf16[32,2,1920]{2,1,0:T(2,128)(2,1)S(1)}, u32[]{:S(2)}, u32[]{:S(2)}) collective-permute-start(bf16[32,2,1920]{2,1,0:T(2,128)(2,1)S(1)} %all_to_all.27.mine_ref), channel_id=1, source_target_pairs={{0,1},{1,0},{2,3},{3,2},{4,5},{5,4},{6,7},{7,6},{8,9},{9,8},{10,11... | collective-permute-start | bytes 737288 | tf_op jit(solution)/shard_map/ppermute | solution.py:30
  95.9 1.1 %collective-permute-done.1.theirs_ref = bf16[32,2,1920]{2,1,0:T(2,128)(2,1)S(1)} collective-permute-done((bf16[32,2,1920]{2,1,0:T(2,128)(2,1)S(1)}, bf16[32,2,1920]{2,1,0:T(2,128)(2,1)S(1)}, u32[]{:S(2)}, u32[]{:S(2)}) %collective-permute-start.1) | collective-permute-done | bytes 245792 | tf_op jit(solution)/shard_map/ppermute | solution.py:30
  97.0 1.9 %shard_map.93 = f32[64,384]{1,0:T(8,128)} custom-call(s32[1,1]{1,0:T(1,128)} %bitcast.core_ref, bf16[32,2,1920]{2,1,0:T(2,128)(2,1)S(1)} %all_to_all.27.mine_ref, bf16[32,2,1920]{2,1,0:T(2,128)(2,1)S(1)} %collective-permute-done.1.theirs_ref, f32[64,384]{1,0:T(8,128)S(1)} %get-tuple-element.28.field_ref, bf16[768,384]{1,0:T(8,128)(2,1)S(1)} %bitcast.36), custom_call_target="tpu_custom_call" | custom-call | tf_op jit(solution)/shard_map/pallas_call | solution.py:40
  (9 shorter events, 0.1 us)
Async XLA Ops:
  0.0 0.7 copy-start.5
  1.6 12.4 %copy-start = (bf16[3,256,384]{2,1,0:T(8,128)(2,1)S(1)}, bf16[3,256,384]{2,1,0:T(8,128)(2,1)}, u32[]{:S(2)}) copy-start(bf16[3,256,384]{2,1,0:T(8,128)(2,1)} %param.14) | copy-start | bytes 1769476
  1.6 12.4 %copy-start.1 = (bf16[3,256,384]{2,1,0:T(8,128)(2,1)S(1)}, bf16[3,256,384]{2,1,0:T(8,128)(2,1)}, u32[]{:S(2)}) copy-start(bf16[3,256,384]{2,1,0:T(8,128)(2,1)} %param.13) | copy-start | bytes 1769476
  2.4 21.7 %all-to-all-start = ((bf16[64,4,128]{2,1,0:T(4,128)(2,1)}), bf16[64,4,128]{2,1,0:T(4,128)(2,1)S(1)}, u32[]{:S(2)}, u32[]{:S(2)}) async-start(bf16[64,4,128]{2,1,0:T(4,128)(2,1)} %pad_maximum_fusion.1), calls=%async_computation | async-start | bytes 131072 | tf_op jit(solution)/shard_map/all_to_all | solution.py:34
  14.0 1.0 %slice-start = ((bf16[3,256,384]{2,1,0:T(8,128)(2,1)}), bf16[2,256,384]{2,1,0:T(8,128)(2,1)S(1)}, s32[]{:S(2)}) async-start(bf16[3,256,384]{2,1,0:T(8,128)(2,1)} %param.14), calls=%async_computation.5 | async-start | bytes 786432 | tf_op jit(solution)/shard_map/slice | solution.py:180
  15.5 14.3 %copy-start.4 = (bf16[2,256,512]{2,1,0:T(8,128)(2,1)S(1)}, bf16[2,256,512]{2,1,0:T(8,128)(2,1)}, u32[]{:S(2)}) copy-start(bf16[2,256,512]{2,1,0:T(8,128)(2,1)} %param.15) | copy-start | bytes 1572868
  15.5 15.3 %collective-permute-start = (bf16[256,384]{1,0:T(8,128)(2,1)S(1)}, bf16[256,384]{1,0:T(8,128)(2,1)S(1)}, u32[]{:S(2)}, u32[]{:S(2)}) collective-permute-start(bf16[256,384]{1,0:T(8,128)(2,1)S(1)} %get-tuple-element.23), channel_id=1, source_target_pairs={{0,1},{1,0},{2,3},{3,2},{4,5},{5,4},{6,7},{7,6},{8,9},{9,8},{10,11... | collective-permute-start | bytes 589832 | tf_op jit(solution)/shard_map/ppermute | solution.py:30
  25.3 15.2 %all-to-all-start.1 = ((bf16[64,2,384]{2,1,0:T(2,128)(2,1)}), bf16[64,2,384]{2,1,0:T(2,128)(2,1)S(1)}, u32[]{:S(2)}, u32[]{:S(2)}) async-start(bf16[64,2,384]{2,1,0:T(2,128)(2,1)} %reshape.69), calls=%async_computation.1 | async-start | bytes 196608 | tf_op jit(solution)/shard_map/all_to_all | solution.py:34
  30.7 9.7 %copy-start.2 = (bf16[3,384,384]{2,1,0:T(8,128)(2,1)S(1)}, bf16[3,384,384]{2,1,0:T(8,128)(2,1)}, u32[]{:S(2)}) copy-start(bf16[3,384,384]{2,1,0:T(8,128)(2,1)} %leaf_ref.1) | copy-start | bytes 2654212
  58.6 17.3 %copy-start.3 = (bf16[1,256,512]{2,1,0:T(8,128)(2,1)S(1)}, bf16[1,256,512]{2,1,0:T(8,128)(2,1)}, u32[]{:S(2)}) copy-start(bf16[1,256,512]{2,1,0:T(8,128)(2,1)} %low_ref.1) | copy-start | bytes 786436
  90.3 6.7 %collective-permute-start.1 = (bf16[32,2,1920]{2,1,0:T(2,128)(2,1)S(1)}, bf16[32,2,1920]{2,1,0:T(2,128)(2,1)S(1)}, u32[]{:S(2)}, u32[]{:S(2)}) collective-permute-start(bf16[32,2,1920]{2,1,0:T(2,128)(2,1)S(1)} %all_to_all.27.mine_ref), channel_id=1, source_target_pairs={{0,1},{1,0},{2,3},{3,2},{4,5},{5,4},{6,7},{7,6},{8,9},{9,8},{10,11... | collective-permute-start | bytes 737288 | tf_op jit(solution)/shard_map/ppermute | solution.py:30
